TPU v7x, 512 devices: a whole 4x8x8 slice. The times are simulated.
512 devices in a mesh: head: 8 (over x, y_lo), ctx: 64 (over y_hi, z, core).
Axes of the slice: x: 4, y: 8 (y_hi: 4, y_lo: 2; y = y_hi * 2 + y_lo), z: 8, core: 2. Of those that a mesh axis runs over, the one named last changes fastest.
Arguments:
- merged_qkv: bfloat16 [16384, 10240], P(('ctx', 'head')), may hold values from -8.5 to 8.5
- out_grads: bfloat16 [16384, 8192], P(('ctx', 'head')), may hold values from -6 to 6
- doc_lengths: int32 [64], replicated, may hold values from 1 to 1536, 16384 in all
Outputs:
- qkv_grads: bfloat16 [16384, 10240], P(('ctx', 'head'))
Inputs may be any that keep to these rules, and one draw needn't show every extreme that they name: `doc_lengths`: the lengths sum to 16384; the largest is exactly 1536.
All inputs are finite; a program needn't handle non-finite values.
Results may differ from a plain program's by a relative error of at most 0.0078.
Values may be sent and summed in bfloat16 or wider, within the bound.
A program may use at most 64 MiB of HBM per device.

v0:
```python
from functools import partial

import jax
import jax.numpy as jnp
from jax import lax
from jax.sharding import PartitionSpec as P

Q_HEADS = 64
KV_HEADS = 8
HEAD_DIM = 128
REACH = 6


def from_behind(value, axis, steps):
    count = lax.axis_size(axis)
    initial, last = (max(0, -steps), min(count, count - steps))
    return lax.ppermute(value, axis, [(source, source + steps) for source in range(initial, last)])


def doc_of(bounds, positions):
    return jnp.sum((bounds[None, :] <= positions[:, None]).astype(jnp.int32), axis=1)


def one_head(key_rows, value_rows, visible, scaling, running, head_pair):
    query_head, grad_head = head_pair
    raw_score = (
        jnp.einsum("qd,kd->qk", query_head, key_rows, preferred_element_type=jnp.float32) * scaling
    )
    raw_score = jnp.where(visible, raw_score, -jnp.inf)
    row_max = jnp.max(raw_score, axis=1, keepdims=True)
    log_total = row_max + jnp.log(jnp.sum(jnp.exp(raw_score - row_max), axis=1, keepdims=True))
    prob_full = jnp.exp(raw_score - log_total)
    prob_half = prob_full.astype(jnp.bfloat16)
    output = jnp.einsum("qk,kd->qd", prob_half, value_rows, preferred_element_type=jnp.float32)
    row_delta = jnp.sum(grad_head.astype(jnp.float32) * output, axis=1, keepdims=True)
    grad_prob = jnp.einsum("qd,kd->qk", grad_head, value_rows, preferred_element_type=jnp.float32)
    grad_score = (prob_full * (grad_prob - row_delta) * scaling).astype(jnp.bfloat16)
    grad_query = jnp.einsum(
        "qk,kd->qd", grad_score, key_rows, preferred_element_type=jnp.float32
    ).astype(jnp.bfloat16)
    grad_key = running[0] + jnp.einsum(
        "qk,qd->kd", grad_score, query_head, preferred_element_type=jnp.float32
    )
    grad_value = running[1] + jnp.einsum(
        "qk,qd->kd", prob_half, grad_head, preferred_element_type=jnp.float32
    )
    return ((grad_key, grad_value), grad_query)


def per_device(merged_qkv, out_grads, doc_lengths):
    inputs, grads_in = (
        lax.all_to_all(merged_qkv, "head", split_axis=1, concat_axis=0, tiled=True),
        lax.all_to_all(out_grads, "head", split_axis=1, concat_axis=0, tiled=True),
    )
    tok_rows = inputs.shape[0]
    group_q = Q_HEADS // KV_HEADS
    head_dim = HEAD_DIM
    groups = inputs.shape[1] // ((group_q + 2) * head_dim)
    scaling = head_dim ** (-0.5)
    merged_view = inputs.reshape(tok_rows, groups, group_q + 2, head_dim)
    queries = jnp.transpose(merged_view[:, :, :group_q], (1, 2, 0, 3))
    grad_heads = jnp.transpose(grads_in.reshape(tok_rows, groups, group_q, head_dim), (1, 2, 0, 3))
    local_pairs = jnp.stack([merged_view[:, :, group_q], merged_view[:, :, group_q + 1]])
    ctx_index = lax.axis_index("ctx")
    first_row = ctx_index * tok_rows
    bounds = jnp.cumsum(doc_lengths)
    row_iota = jnp.arange(tok_rows, dtype=jnp.int32)
    query_pos = first_row + row_iota
    query_doc = doc_of(bounds, query_pos)
    remote = []
    moving = local_pairs
    for r in range(REACH):
        moving = from_behind(moving, "ctx", 1)
        remote.append(moving)
    blocks = [local_pairs] + remote

    def attend(reach_now):
        key_order = list(range(reach_now, -1, -1))
        key_value = jnp.concatenate([blocks[r] for r in key_order], axis=1)
        key_pos = jnp.concatenate([first_row - r * tok_rows + row_iota for r in key_order])
        visible = query_doc[:, None] == doc_of(bounds, key_pos)[None, :]
        visible = visible & (key_pos[None, :] <= query_pos[:, None]) & (key_pos >= 0)[None, :]
        key_groups = jnp.transpose(key_value[0], (1, 0, 2))
        value_groups = jnp.transpose(key_value[1], (1, 0, 2))
        key_count = key_value.shape[1]

        def per_group(group_args):
            query_grp, grad_grp, key_grp, value_grp = group_args
            zero_grads = jnp.zeros((key_count, head_dim), jnp.float32)
            (grad_key, grad_value), grad_query = lax.scan(
                partial(one_head, key_grp, value_grp, visible, scaling),
                (zero_grads, zero_grads),
                (query_grp, grad_grp),
            )
            return (grad_query, grad_key, grad_value)

        grad_query, grad_key, grad_value = lax.map(
            per_group, (queries, grad_heads, key_groups, value_groups)
        )
        grad_query = jnp.transpose(grad_query, (2, 0, 1, 3))
        grad_pairs = jnp.transpose(jnp.stack([grad_key, grad_value]), (0, 2, 1, 3))
        pieces = [jnp.zeros((2, tok_rows, groups, head_dim), jnp.float32) for r in range(REACH + 1)]
        for i, r in enumerate(key_order):
            pieces[r] = grad_pairs[:, i * tok_rows : (i + 1) * tok_rows]
        return (grad_query, tuple(pieces))

    grad_query, pieces = attend(REACH)
    home_grads = pieces[REACH]
    for r in range(REACH - 1, -1, -1):
        home_grads = from_behind(home_grads, "ctx", -1) + pieces[r]
    home_half = home_grads.astype(jnp.bfloat16)
    joined = jnp.concatenate(
        [grad_query, home_half[0][:, :, None], home_half[1][:, :, None]], axis=2
    )
    joined = joined.reshape(tok_rows, groups * (group_q + 2) * head_dim)
    return lax.all_to_all(joined, "head", split_axis=0, concat_axis=1, tiled=True)


def solution(mesh):
    placed = (P(("ctx", "head"), None), P(("ctx", "head"), None), P())
    return jax.shard_map(
        per_device, mesh=mesh, in_specs=placed, out_specs=P(("ctx", "head"), None), check_vma=False
    )
```

profile of v0, /device:TPU:32, one launch (start us, length us, event | category | flops | bytes accessed | tf_op | source)
XLA Modules:
  0.0 265.5 jit_solution(4397246302511979714)
XLA Ops:
  0.0 2.0 copy.44
  2.0 4.4 %all-to-all-start = ((bf16[32,8,1280]{2,0,1:T(8,128)(2,1)}), bf16[32,8,1280]{2,0,1:T(8,128)(2,1)S(1)}, u32[]{:S(2)}, u32[]{:S(2)}) async-start(bf16[32,8,1280]{2,0,1:T(8,128)(2,1)} %bitcast.69), calls=%async_computation | async-start | bytes 1310720 | tf_op jit(solution)/shard_map/all_to_all | solution.py:52
  7.3 10.6 %all-to-all-done = bf16[32,8,1280]{2,0,1:T(8,128)(2,1)S(1)} async-done(((bf16[32,8,1280]{2,0,1:T(8,128)(2,1)}), bf16[32,8,1280]{2,0,1:T(8,128)(2,1)S(1)}, u32[]{:S(2)}, u32[]{:S(2)}) %all-to-all-start) | async-done | bytes 655392 | tf_op jit(solution)/shard_map/all_to_all | solution.py:52
  17.9 3.6 %all-to-all-start.1 = ((bf16[32,8,1024]{2,0,1:T(8,128)(2,1)}), bf16[32,8,1024]{2,0,1:T(8,128)(2,1)S(1)}, u32[]{:S(2)}, u32[]{:S(2)}) async-start(bf16[32,8,1024]{2,0,1:T(8,128)(2,1)} %bitcast.70), calls=%async_computation.1 | async-start | bytes 1048576 | tf_op jit(solution)/shard_map/all_to_all | solution.py:53
  22.2 1.9 collective-permute-start
  24.2 14.3 %collective-permute-done = bf16[2,256,1,128]{3,1,2,0:T(8,128)(2,1)S(1)} collective-permute-done((bf16[2,256,1,128]{3,1,2,0:T(8,128)(2,1)S(1)}, bf16[2,256,1,128]{3,1,2,0:T(8,128)(2,1)S(1)}, u32[]{:S(2)}, u32[]{:S(2)}) %collective-permute-start) | collective-permute-done | bytes 131104 | tf_op jit(solution)/shard_map/ppermute | solution.py:17
  38.5 1.9 collective-permute-start.1
  40.4 8.5 %collective-permute-done.1 = bf16[2,256,1,128]{3,1,2,0:T(8,128)(2,1)S(1)} collective-permute-done((bf16[2,256,1,128]{3,1,2,0:T(8,128)(2,1)S(1)}, bf16[2,256,1,128]{3,1,2,0:T(8,128)(2,1)S(1)}, u32[]{:S(2)}, u32[]{:S(2)}) %collective-permute-start.1) | collective-permute-done | bytes 131104 | tf_op jit(solution)/shard_map/ppermute | solution.py:17
  49.0 1.9 collective-permute-start.2
  51.3 8.2 %collective-permute-done.2 = bf16[2,256,1,128]{3,1,2,0:T(8,128)(2,1)S(1)} collective-permute-done((bf16[2,256,1,128]{3,1,2,0:T(8,128)(2,1)S(1)}, bf16[2,256,1,128]{3,1,2,0:T(8,128)(2,1)S(1)}, u32[]{:S(2)}, u32[]{:S(2)}) %collective-permute-start.2) | collective-permute-done | bytes 131104 | tf_op jit(solution)/shard_map/ppermute | solution.py:17
  59.5 1.9 collective-permute-start.3
  62.0 8.1 %collective-permute-done.3 = bf16[2,256,1,128]{3,1,2,0:T(8,128)(2,1)} collective-permute-done((bf16[2,256,1,128]{3,1,2,0:T(8,128)(2,1)S(1)}, bf16[2,256,1,128]{3,1,2,0:T(8,128)(2,1)}, u32[]{:S(2)}, u32[]{:S(2)}) %collective-permute-start.3) | collective-permute-done | bytes 131104 | tf_op jit(solution)/shard_map/ppermute | solution.py:17
  70.1 1.9 collective-permute-start.4
  74.1 6.8 %collective-permute-done.4 = bf16[2,256,1,128]{3,1,2,0:T(8,128)(2,1)} collective-permute-done((bf16[2,256,1,128]{3,1,2,0:T(8,128)(2,1)}, bf16[2,256,1,128]{3,1,2,0:T(8,128)(2,1)}, u32[]{:S(2)}, u32[]{:S(2)}) %collective-permute-start.4) | collective-permute-done | bytes 131104 | tf_op jit(solution)/shard_map/ppermute | solution.py:17
  80.9 1.9 collective-permute-start.5
  83.8 7.8 %collective-permute-done.5 = bf16[2,256,1,128]{3,1,2,0:T(8,128)(2,1)S(1)} collective-permute-done((bf16[2,256,1,128]{3,1,2,0:T(8,128)(2,1)}, bf16[2,256,1,128]{3,1,2,0:T(8,128)(2,1)S(1)}, u32[]{:S(2)}, u32[]{:S(2)}) %collective-permute-start.5) | collective-permute-done | bytes 131104 | tf_op jit(solution)/shard_map/ppermute | solution.py:17
  94.4 84.0 %while.26 = (s32[]{:T(128)}, f32[1792,128]{1,0:T(8,128)S(1)}, f32[1792,128]{1,0:T(8,128)}, bf16[8,256,128]{2,1,0:T(8,128)(2,1)}, bf16[8,256,128]{2,1,0:T(8,128)(...) while((s32[]{:T(128)}, f32[1792,128]{1,0:T(8,128)S(1)}, ...), condition=%wide.region_7.8_spmd.clone, body=%wide.region_3.7_spmd.clone.sunk | while | flops 713948672 | bytes 19693240 | solution.py:90
  94.4 1.8 fusion.59
  96.6 2.4 convolution_add_fusion.5
  101.9 1.7 convolution_add_fusion.4
  104.6 1.8 fusion.59
  106.8 2.7 %convolution_add_fusion.5 = f32[1792,128]{1,0:T(8,128)} fusion(f32[1792,128]{1,0:T(8,128)} %get-tuple-element.323, pred[]{:T(512)S(6)} %compare.3, bf16[8,256,128]{1,2,0:T(8,128)(2,1)} %get-tuple-element.342, s32[]{:T(128)} %get-tuple-element.321, f32[256,1792]{1,0:T(8,128)S(1)} %get-tuple-element.304, f32[256]{0:T(256)S(1)} %log_add_fusion.2), kind=kOutput, calls=%fused_computation.7.clone.1 | convolution fusion | flops 118816768 | bytes 3737089 | tf_op jit(solution)/shard_map/while/body/eval_jaxpr/while/body/eval_jaxpr/qk,qd->kd/dot_general | solution.py:44
  112.4 1.7 convolution_add_fusion.4
  115.1 1.8 fusion.59
  117.4 2.7 %convolution_add_fusion.5 = f32[1792,128]{1,0:T(8,128)} fusion(f32[1792,128]{1,0:T(8,128)} %get-tuple-element.323, pred[]{:T(512)S(6)} %compare.3, bf16[8,256,128]{1,2,0:T(8,128)(2,1)} %get-tuple-element.342, s32[]{:T(128)} %get-tuple-element.321, f32[256,1792]{1,0:T(8,128)S(1)} %get-tuple-element.304, f32[256]{0:T(256)S(1)} %log_add_fusion.2), kind=kOutput, calls=%fused_computation.7.clone.1 | convolution fusion | flops 118816768 | bytes 3737089 | tf_op jit(solution)/shard_map/while/body/eval_jaxpr/while/body/eval_jaxpr/qk,qd->kd/dot_general | solution.py:44
  125.7 1.8 fusion.59
  127.9 2.7 %convolution_add_fusion.5 = f32[1792,128]{1,0:T(8,128)} fusion(f32[1792,128]{1,0:T(8,128)} %get-tuple-element.323, pred[]{:T(512)S(6)} %compare.3, bf16[8,256,128]{1,2,0:T(8,128)(2,1)} %get-tuple-element.342, s32[]{:T(128)} %get-tuple-element.321, f32[256,1792]{1,0:T(8,128)S(1)} %get-tuple-element.304, f32[256]{0:T(256)S(1)} %log_add_fusion.2), kind=kOutput, calls=%fused_computation.7.clone.1 | convolution fusion | flops 118816768 | bytes 3737089 | tf_op jit(solution)/shard_map/while/body/eval_jaxpr/while/body/eval_jaxpr/qk,qd->kd/dot_general | solution.py:44
  136.2 1.8 fusion.59
  138.5 2.7 %convolution_add_fusion.5 = f32[1792,128]{1,0:T(8,128)} fusion(f32[1792,128]{1,0:T(8,128)} %get-tuple-element.323, pred[]{:T(512)S(6)} %compare.3, bf16[8,256,128]{1,2,0:T(8,128)(2,1)} %get-tuple-element.342, s32[]{:T(128)} %get-tuple-element.321, f32[256,1792]{1,0:T(8,128)S(1)} %get-tuple-element.304, f32[256]{0:T(256)S(1)} %log_add_fusion.2), kind=kOutput, calls=%fused_computation.7.clone.1 | convolution fusion | flops 118816768 | bytes 3737089 | tf_op jit(solution)/shard_map/while/body/eval_jaxpr/while/body/eval_jaxpr/qk,qd->kd/dot_general | solution.py:44
  146.8 1.8 fusion.59
  149.0 2.7 %convolution_add_fusion.5 = f32[1792,128]{1,0:T(8,128)} fusion(f32[1792,128]{1,0:T(8,128)} %get-tuple-element.323, pred[]{:T(512)S(6)} %compare.3, bf16[8,256,128]{1,2,0:T(8,128)(2,1)} %get-tuple-element.342, s32[]{:T(128)} %get-tuple-element.321, f32[256,1792]{1,0:T(8,128)S(1)} %get-tuple-element.304, f32[256]{0:T(256)S(1)} %log_add_fusion.2), kind=kOutput, calls=%fused_computation.7.clone.1 | convolution fusion | flops 118816768 | bytes 3737089 | tf_op jit(solution)/shard_map/while/body/eval_jaxpr/while/body/eval_jaxpr/qk,qd->kd/dot_general | solution.py:44
  157.4 1.8 fusion.59
  159.6 2.7 %convolution_add_fusion.5 = f32[1792,128]{1,0:T(8,128)} fusion(f32[1792,128]{1,0:T(8,128)} %get-tuple-element.323, pred[]{:T(512)S(6)} %compare.3, bf16[8,256,128]{1,2,0:T(8,128)(2,1)} %get-tuple-element.342, s32[]{:T(128)} %get-tuple-element.321, f32[256,1792]{1,0:T(8,128)S(1)} %get-tuple-element.304, f32[256]{0:T(256)S(1)} %log_add_fusion.2), kind=kOutput, calls=%fused_computation.7.clone.1 | convolution fusion | flops 118816768 | bytes 3737089 | tf_op jit(solution)/shard_map/while/body/eval_jaxpr/while/body/eval_jaxpr/qk,qd->kd/dot_general | solution.py:44
  167.9 1.8 fusion.59
  170.1 2.7 %convolution_add_fusion.5 = f32[1792,128]{1,0:T(8,128)} fusion(f32[1792,128]{1,0:T(8,128)} %get-tuple-element.323, pred[]{:T(512)S(6)} %compare.3, bf16[8,256,128]{1,2,0:T(8,128)(2,1)} %get-tuple-element.342, s32[]{:T(128)} %get-tuple-element.321, f32[256,1792]{1,0:T(8,128)S(1)} %get-tuple-element.304, f32[256]{0:T(256)S(1)} %log_add_fusion.2), kind=kOutput, calls=%fused_computation.7.clone.1 | convolution fusion | flops 118816768 | bytes 3737089 | tf_op jit(solution)/shard_map/while/body/eval_jaxpr/while/body/eval_jaxpr/qk,qd->kd/dot_general | solution.py:44
  179.8 1.9 collective-permute-start.6
  181.7 3.9 %collective-permute-done.6 = f32[2,256,1,128]{3,1,2,0:T(8,128)S(1)} collective-permute-done((f32[2,256,1,128]{3,1,2,0:T(8,128)S(1)}, f32[2,256,1,128]{3,1,2,0:T(8,128)S(1)}, u32[]{:S(2)}, u32[]{:S(2)}) %collective-permute-start.6) | collective-permute-done | bytes 262176 | tf_op jit(solution)/shard_map/ppermute | solution.py:17
  185.7 8.1 %collective-permute-start.7 = (f32[2,256,1,128]{3,1,2,0:T(8,128)S(1)}, f32[2,256,1,128]{3,1,2,0:T(8,128)S(1)}, u32[]{:S(2)}, u32[]{:S(2)}) collective-permute-start(f32[2,256,1,128]{3,1,2,0:T(8,128)S(1)} %slice_add_fusion.5), channel_id=1, source_target_pairs={{1,0},{2,1},{3,2},{4,3},{5,4},{6,5},{7,6},{8,7},{9,8},{10,9},{11,1... | collective-permute-start | bytes 786440 | tf_op jit(solution)/shard_map/ppermute | solution.py:17
  193.8 6.7 %collective-permute-done.7 = f32[2,256,1,128]{3,1,2,0:T(8,128)S(1)} collective-permute-done((f32[2,256,1,128]{3,1,2,0:T(8,128)S(1)}, f32[2,256,1,128]{3,1,2,0:T(8,128)S(1)}, u32[]{:S(2)}, u32[]{:S(2)}) %collective-permute-start.7) | collective-permute-done | bytes 262176 | tf_op jit(solution)/shard_map/ppermute | solution.py:17
  200.5 8.2 %collective-permute-start.8 = (f32[2,256,1,128]{3,1,2,0:T(8,128)S(1)}, f32[2,256,1,128]{3,1,2,0:T(8,128)S(1)}, u32[]{:S(2)}, u32[]{:S(2)}) collective-permute-start(f32[2,256,1,128]{3,1,2,0:T(8,128)S(1)} %slice_add_fusion.4), channel_id=1, source_target_pairs={{1,0},{2,1},{3,2},{4,3},{5,4},{6,5},{7,6},{8,7},{9,8},{10,9},{11,1... | collective-permute-start | bytes 786440 | tf_op jit(solution)/shard_map/ppermute | solution.py:17
  208.7 5.4 %collective-permute-done.8 = f32[2,256,1,128]{3,1,2,0:T(8,128)S(1)} collective-permute-done((f32[2,256,1,128]{3,1,2,0:T(8,128)S(1)}, f32[2,256,1,128]{3,1,2,0:T(8,128)S(1)}, u32[]{:S(2)}, u32[]{:S(2)}) %collective-permute-start.8) | collective-permute-done | bytes 262176 | tf_op jit(solution)/shard_map/ppermute | solution.py:17
  214.1 8.0 %collective-permute-start.9 = (f32[2,256,1,128]{3,1,2,0:T(8,128)S(1)}, f32[2,256,1,128]{3,1,2,0:T(8,128)S(1)}, u32[]{:S(2)}, u32[]{:S(2)}) collective-permute-start(f32[2,256,1,128]{3,1,2,0:T(8,128)S(1)} %slice_add_fusion.3), channel_id=1, source_target_pairs={{1,0},{2,1},{3,2},{4,3},{5,4},{6,5},{7,6},{8,7},{9,8},{10,9},{11,1... | collective-permute-start | bytes 786440 | tf_op jit(solution)/shard_map/ppermute | solution.py:17
  222.2 4.0 %collective-permute-done.9 = f32[2,256,1,128]{3,1,2,0:T(8,128)S(1)} collective-permute-done((f32[2,256,1,128]{3,1,2,0:T(8,128)S(1)}, f32[2,256,1,128]{3,1,2,0:T(8,128)S(1)}, u32[]{:S(2)}, u32[]{:S(2)}) %collective-permute-start.9) | collective-permute-done | bytes 262176 | tf_op jit(solution)/shard_map/ppermute | solution.py:17
  226.2 8.0 %collective-permute-start.10 = (f32[2,256,1,128]{3,1,2,0:T(8,128)S(1)}, f32[2,256,1,128]{3,1,2,0:T(8,128)S(1)}, u32[]{:S(2)}, u32[]{:S(2)}) collective-permute-start(f32[2,256,1,128]{3,1,2,0:T(8,128)S(1)} %slice_add_fusion.2), channel_id=1, source_target_pairs={{1,0},{2,1},{3,2},{4,3},{5,4},{6,5},{7,6},{8,7},{9,8},{10,9},{11,1... | collective-permute-start | bytes 786440 | tf_op jit(solution)/shard_map/ppermute | solution.py:17
  234.2 3.9 %collective-permute-done.10 = f32[2,256,1,128]{3,1,2,0:T(8,128)S(1)} collective-permute-done((f32[2,256,1,128]{3,1,2,0:T(8,128)S(1)}, f32[2,256,1,128]{3,1,2,0:T(8,128)S(1)}, u32[]{:S(2)}, u32[]{:S(2)}) %collective-permute-start.10) | collective-permute-done | bytes 262176 | tf_op jit(solution)/shard_map/ppermute | solution.py:17
  238.2 8.1 %collective-permute-start.11 = (f32[2,256,1,128]{3,1,2,0:T(8,128)S(1)}, f32[2,256,1,128]{3,1,2,0:T(8,128)S(1)}, u32[]{:S(2)}, u32[]{:S(2)}) collective-permute-start(f32[2,256,1,128]{3,1,2,0:T(8,128)S(1)} %slice_add_fusion.1), channel_id=1, source_target_pairs={{1,0},{2,1},{3,2},{4,3},{5,4},{6,5},{7,6},{8,7},{9,8},{10,9},{11,1... | collective-permute-start | bytes 786440 | tf_op jit(solution)/shard_map/ppermute | solution.py:17
  246.3 3.9 %collective-permute-done.11 = f32[2,256,1,128]{3,1,2,0:T(8,128)S(1)} collective-permute-done((f32[2,256,1,128]{3,1,2,0:T(8,128)S(1)}, f32[2,256,1,128]{3,1,2,0:T(8,128)S(1)}, u32[]{:S(2)}, u32[]{:S(2)}) %collective-permute-start.11) | collective-permute-done | bytes 262176 | tf_op jit(solution)/shard_map/ppermute | solution.py:17
  251.2 13.4 %all_to_all.51 = bf16[8,32,1280]{2,1,0:T(8,128)(2,1)S(1)} all-to-all(bf16[8,32,1280]{2,1,0:T(8,128)(2,1)S(1)} %all_to_all.44), channel_id=1, replica_groups=mesh['head'=8,'ctx'=64] {'head'}, dimensions={0} | all-to-all | bytes 1310720 | tf_op jit(solution)/shard_map/all_to_all | solution.py:116
  (118 shorter events, 56.0 us)
Async XLA Ops:
  0.0 6.4 %copy-start.1 = (bf16[32,8192]{1,0:T(8,128)(2,1)S(1)}, bf16[32,8192]{1,0:T(8,128)(2,1)}, u32[]{:S(2)}) copy-start(bf16[32,8192]{1,0:T(8,128)(2,1)} %param.6) | copy-start | bytes 1572868
  2.0 15.9 %all-to-all-start = ((bf16[32,8,1280]{2,0,1:T(8,128)(2,1)}), bf16[32,8,1280]{2,0,1:T(8,128)(2,1)S(1)}, u32[]{:S(2)}, u32[]{:S(2)}) async-start(bf16[32,8,1280]{2,0,1:T(8,128)(2,1)} %bitcast.69), calls=%async_computation | async-start | bytes 1310720 | tf_op jit(solution)/shard_map/all_to_all | solution.py:52
  17.9 33.0 %copy-start.4 = (s32[64]{0:T(128)S(1)}, s32[64]{0:T(128)}, u32[]{:S(2)}) copy-start(s32[64]{0:T(128)} %param.7) | copy-start | bytes 772
  17.9 54.9 %all-to-all-start.1 = ((bf16[32,8,1024]{2,0,1:T(8,128)(2,1)}), bf16[32,8,1024]{2,0,1:T(8,128)(2,1)S(1)}, u32[]{:S(2)}, u32[]{:S(2)}) async-start(bf16[32,8,1024]{2,0,1:T(8,128)(2,1)} %bitcast.70), calls=%async_computation.1 | async-start | bytes 1048576 | tf_op jit(solution)/shard_map/all_to_all | solution.py:53
  22.2 16.3 %collective-permute-start = (bf16[2,256,1,128]{3,1,2,0:T(8,128)(2,1)S(1)}, bf16[2,256,1,128]{3,1,2,0:T(8,128)(2,1)S(1)}, u32[]{:S(2)}, u32[]{:S(2)}) collective-permute-start(bf16[2,256,1,128]{3,1,2,0:T(8,128)(2,1)S(1)} %pad_maximum_fusion.1), channel_id=1, source_target_pairs={{0,1},{1,2},{2,3},{3,4},{4,5},{5,6},{6,7},{7,8},{8,9},{9,10},{10,1... | collective-permute-start | bytes 393224 | tf_op jit(solution)/shard_map/ppermute | solution.py:17
  38.5 10.5 %collective-permute-start.1 = (bf16[2,256,1,128]{3,1,2,0:T(8,128)(2,1)S(1)}, bf16[2,256,1,128]{3,1,2,0:T(8,128)(2,1)S(1)}, u32[]{:S(2)}, u32[]{:S(2)}) collective-permute-start(bf16[2,256,1,128]{3,1,2,0:T(8,128)(2,1)S(1)} %collective-permute-done), channel_id=1, source_target_pairs={{0,1},{1,2},{2,3},{3,4},{4,5},{5,6},{6,7},{7,8},{8,9},{9,10},{10,1... | collective-permute-start | bytes 393224 | tf_op jit(solution)/shard_map/ppermute | solution.py:17
  49.0 10.5 %collective-permute-start.2 = (bf16[2,256,1,128]{3,1,2,0:T(8,128)(2,1)S(1)}, bf16[2,256,1,128]{3,1,2,0:T(8,128)(2,1)S(1)}, u32[]{:S(2)}, u32[]{:S(2)}) collective-permute-start(bf16[2,256,1,128]{3,1,2,0:T(8,128)(2,1)S(1)} %collective-permute-done.1), channel_id=1, source_target_pairs={{0,1},{1,2},{2,3},{3,4},{4,5},{5,6},{6,7},{7,8},{8,9},{9,10},{10,1... | collective-permute-start | bytes 393224 | tf_op jit(solution)/shard_map/ppermute | solution.py:17
  51.2 21.6 %copy-start.3 = (s32[256]{0:T(256)}, s32[256]{0:T(256)S(1)}, u32[]{:S(2)}) copy-start(s32[256]{0:T(256)S(1)} %get-tuple-element.316) | copy-start | bytes 3076
  59.5 10.6 %collective-permute-start.3 = (bf16[2,256,1,128]{3,1,2,0:T(8,128)(2,1)S(1)}, bf16[2,256,1,128]{3,1,2,0:T(8,128)(2,1)}, u32[]{:S(2)}, u32[]{:S(2)}) collective-permute-start(bf16[2,256,1,128]{3,1,2,0:T(8,128)(2,1)S(1)} %collective-permute-done.2), channel_id=1, source_target_pairs={{0,1},{1,2},{2,3},{3,4},{4,5},{5,6},{6,7},{7,8},{8,9},{9,10},{10,1... | collective-permute-start | bytes 393224 | tf_op jit(solution)/shard_map/ppermute | solution.py:17
  70.1 10.8 %collective-permute-start.4 = (bf16[2,256,1,128]{3,1,2,0:T(8,128)(2,1)}, bf16[2,256,1,128]{3,1,2,0:T(8,128)(2,1)}, u32[]{:S(2)}, u32[]{:S(2)}) collective-permute-start(bf16[2,256,1,128]{3,1,2,0:T(8,128)(2,1)} %collective-permute-done.3), channel_id=1, source_target_pairs={{0,1},{1,2},{2,3},{3,4},{4,5},{5,6},{6,7},{7,8},{8,9},{9,10},{10,1... | collective-permute-start | bytes 393224 | tf_op jit(solution)/shard_map/ppermute | solution.py:17
  80.9 10.7 %collective-permute-start.5 = (bf16[2,256,1,128]{3,1,2,0:T(8,128)(2,1)}, bf16[2,256,1,128]{3,1,2,0:T(8,128)(2,1)S(1)}, u32[]{:S(2)}, u32[]{:S(2)}) collective-permute-start(bf16[2,256,1,128]{3,1,2,0:T(8,128)(2,1)} %collective-permute-done.4), channel_id=1, source_target_pairs={{0,1},{1,2},{2,3},{3,4},{4,5},{5,6},{6,7},{7,8},{8,9},{9,10},{10,1... | collective-permute-start | bytes 393224 | tf_op jit(solution)/shard_map/ppermute | solution.py:17
  101.9 1.7 copy-start
  112.4 1.7 copy-start
  123.0 1.7 copy-start
  133.5 1.7 copy-start
  144.1 1.7 copy-start
  154.6 1.7 copy-start
  165.2 1.7 copy-start
  175.7 1.7 copy-start
  179.8 5.8 %collective-permute-start.6 = (f32[2,256,1,128]{3,1,2,0:T(8,128)S(1)}, f32[2,256,1,128]{3,1,2,0:T(8,128)S(1)}, u32[]{:S(2)}, u32[]{:S(2)}) collective-permute-start(f32[2,256,1,128]{3,1,2,0:T(8,128)S(1)} %slice.61), channel_id=1, source_target_pairs={{1,0},{2,1},{3,2},{4,3},{5,4},{6,5},{7,6},{8,7},{9,8},{10,9},{11,1... | collective-permute-start | bytes 786440 | tf_op jit(solution)/shard_map/ppermute | solution.py:17
  185.7 14.8 %collective-permute-start.7 = (f32[2,256,1,128]{3,1,2,0:T(8,128)S(1)}, f32[2,256,1,128]{3,1,2,0:T(8,128)S(1)}, u32[]{:S(2)}, u32[]{:S(2)}) collective-permute-start(f32[2,256,1,128]{3,1,2,0:T(8,128)S(1)} %slice_add_fusion.5), channel_id=1, source_target_pairs={{1,0},{2,1},{3,2},{4,3},{5,4},{6,5},{7,6},{8,7},{9,8},{10,9},{11,1... | collective-permute-start | bytes 786440 | tf_op jit(solution)/shard_map/ppermute | solution.py:17
  200.5 49.7 %copy-start.2 = (bf16[8,256,128]{2,1,0:T(8,128)(2,1)S(1)}, bf16[8,256,128]{2,1,0:T(8,128)(2,1)}, u32[]{:S(2)}) copy-start(bf16[8,256,128]{2,1,0:T(8,128)(2,1)} %get-tuple-element.81) | copy-start | bytes 1572868
  200.5 13.6 %collective-permute-start.8 = (f32[2,256,1,128]{3,1,2,0:T(8,128)S(1)}, f32[2,256,1,128]{3,1,2,0:T(8,128)S(1)}, u32[]{:S(2)}, u32[]{:S(2)}) collective-permute-start(f32[2,256,1,128]{3,1,2,0:T(8,128)S(1)} %slice_add_fusion.4), channel_id=1, source_target_pairs={{1,0},{2,1},{3,2},{4,3},{5,4},{6,5},{7,6},{8,7},{9,8},{10,9},{11,1... | collective-permute-start | bytes 786440 | tf_op jit(solution)/shard_map/ppermute | solution.py:17
  214.1 12.0 %collective-permute-start.9 = (f32[2,256,1,128]{3,1,2,0:T(8,128)S(1)}, f32[2,256,1,128]{3,1,2,0:T(8,128)S(1)}, u32[]{:S(2)}, u32[]{:S(2)}) collective-permute-start(f32[2,256,1,128]{3,1,2,0:T(8,128)S(1)} %slice_add_fusion.3), channel_id=1, source_target_pairs={{1,0},{2,1},{3,2},{4,3},{5,4},{6,5},{7,6},{8,7},{9,8},{10,9},{11,1... | collective-permute-start | bytes 786440 | tf_op jit(solution)/shard_map/ppermute | solution.py:17
  226.2 12.0 %collective-permute-start.10 = (f32[2,256,1,128]{3,1,2,0:T(8,128)S(1)}, f32[2,256,1,128]{3,1,2,0:T(8,128)S(1)}, u32[]{:S(2)}, u32[]{:S(2)}) collective-permute-start(f32[2,256,1,128]{3,1,2,0:T(8,128)S(1)} %slice_add_fusion.2), channel_id=1, source_target_pairs={{1,0},{2,1},{3,2},{4,3},{5,4},{6,5},{7,6},{8,7},{9,8},{10,9},{11,1... | collective-permute-start | bytes 786440 | tf_op jit(solution)/shard_map/ppermute | solution.py:17
  238.2 12.0 %collective-permute-start.11 = (f32[2,256,1,128]{3,1,2,0:T(8,128)S(1)}, f32[2,256,1,128]{3,1,2,0:T(8,128)S(1)}, u32[]{:S(2)}, u32[]{:S(2)}) collective-permute-start(f32[2,256,1,128]{3,1,2,0:T(8,128)S(1)} %slice_add_fusion.1), channel_id=1, source_target_pairs={{1,0},{2,1},{3,2},{4,3},{5,4},{6,5},{7,6},{8,7},{9,8},{10,9},{11,1... | collective-permute-start | bytes 786440 | tf_op jit(solution)/shard_map/ppermute | solution.py:17
where the time goes:
time: 268 us; the launch traced here: 266 us
  waiting for transfers between devices  92.2 us (34%)
  matrix products  80.3 us (30%)
  starting transfers between devices  61.9 us (23%)
  blocking collectives  13.4 us (5%)
  local copies, waits for them, and re-layouts  10.3 us (4%)
  other arithmetic  6.58 us (2%)
    ppermute x12, waiting for transfers between devices, from_behind(): lax.ppermute(value, axis, [(source, source + steps) for source in range(i...  81.6 us
    ppermute x12, starting transfers between devices, from_behind(): lax.ppermute(value, axis, [(source, source + steps) for source in range(i...  53.8 us
    dot_general x8, matrix products, one_head(): jnp.einsum('qk,qd->kd', prob_half, grad_head, preferred_element_type=jnp....  21.5 us
    dot_general x8, matrix products, one_head(): jnp.einsum('qd,kd->qk', query_head, key_rows, preferred_element_type=jnp....  14.4 us
    all_to_all x1, blocking collectives, per_device(): lax.all_to_all(joined, 'head', split_axis=0, concat_axis=1, tiled=True)  13.4 us
    dot_general x8, matrix products, one_head(): jnp.einsum('qk,qd->kd', grad_score, query_head, preferred_element_type=jn...  13.3 us
    dot_general x8, matrix products, one_head(): jnp.einsum('qd,kd->qk', grad_head, value_rows, preferred_element_type=jnp...  11.6 us
    dot_general x8, matrix products, one_head(): jnp.einsum('qk,kd->qd', prob_half, value_rows, preferred_element_type=jnp...  11.3 us
  transfers between devices with their start and end apart: 14, of which 13 were waited for; matrix products, arithmetic and copies ran while one was open for 2% of the time, Pallas kernels for 0%

commit v1 on v0

v1 whole, which is shorter than its diff:
```python
import functools
import math

import jax
import jax.numpy as jnp
from jax import lax
from jax.experimental import pallas as pl
from jax.experimental.pallas import tpu as pltpu
from jax.sharding import PartitionSpec as P

GROUP_Q = 8
HEAD_DIM = 128
REACH = 6
MESH = pl.DeviceIdType.MESH
SCALE = HEAD_DIM ** -0.5
TO_EXP2 = SCALE * math.log2(math.e)
FAR = 2.0 ** 100
F32, BF16 = jnp.float32, jnp.bfloat16
IN_CHUNKS = 2
HEADS_STEP = 2


def nt(a, b):
    return lax.dot_general(a, b, (((1,), (1,)), ((), ())), preferred_element_type=F32)


def nn(a, b):
    return lax.dot_general(a, b, (((1,), (0,)), ((), ())), preferred_element_type=F32)


def tn(a, b):
    return lax.dot_general(a, b, (((0,), (0,)), ((), ())), preferred_element_type=F32)


def wait_bytes(ref, sem):
    pltpu.make_async_copy(ref, ref, sem).wait()


def kernel(n_head, n_ctx, lens_ref, qkv_ref, grads_ref, out_ref,
           kv, key_doc, query_doc, qb, dob, probs, dprobs, st_m, st_l, st_d, gain, delta,
           dq, home, part, odd_out, odd_in, rail_out, rail_in, stage,
           s_in, r_in, l_in, s_rail, r_rail, s_sib, r_sib, s_grail, r_grail, s_gsib, r_gsib,
           s_out, r_out, l_out):
    rows = qkv_ref.shape[0]
    piece = kv.shape[1]
    width = (GROUP_Q + 2) * HEAD_DIM
    q_width = GROUP_Q * HEAD_DIM
    me = lax.axis_index("head")
    ctx = lax.axis_index("ctx")
    core = lax.rem(ctx, 2)
    sib = ctx + 1 - 2 * core
    after = lax.rem(ctx + 2, n_ctx)
    before = lax.rem(ctx + n_ctx - 2, n_ctx)
    peers = [lax.rem(me + p, n_head) for p in range(1, n_head)]

    barrier = pltpu.get_barrier_semaphore()
    for peer in peers:
        pl.semaphore_signal(barrier, inc=1, device_id={"head": peer}, device_id_type=MESH)
    for other in (sib, after, before):
        pl.semaphore_signal(barrier, inc=1, device_id={"ctx": other}, device_id_type=MESH)
    pl.semaphore_wait(barrier, len(peers) + 3)

    my_rows = pl.ds(pl.multiple_of(me * rows, rows), rows)

    def column(group, first, size):
        return pl.ds(pl.multiple_of(group * width + first, HEAD_DIM), size)

    def grad_column(group, first, size):
        return pl.ds(pl.multiple_of(group * q_width + first, HEAD_DIM), size)

    step_w = q_width // IN_CHUNKS
    sends = [(qkv_ref, lambda g: column(g, q_width, 2 * HEAD_DIM), kv.at[0], pl.ds(0, 2 * HEAD_DIM))]
    for chunk in range(IN_CHUNKS):
        cols = pl.ds(chunk * step_w, step_w)
        sends.append((qkv_ref, lambda g, f=chunk * step_w: column(g, f, step_w), qb, cols))
        sends.append((grads_ref, lambda g, f=chunk * step_w: grad_column(g, f, step_w), dob, cols))
    for i, (src, src_cols, dst, dst_cols) in enumerate(sends):
        for peer in peers:
            pltpu.make_async_remote_copy(
                src_ref=src.at[:, src_cols(peer)], dst_ref=dst.at[my_rows, dst_cols],
                send_sem=s_in.at[i], recv_sem=r_in.at[i],
                device_id={"head": peer}, device_id_type=MESH).start()
        pltpu.make_async_copy(src.at[:, src_cols(me)], dst.at[my_rows, dst_cols], l_in.at[i]).start()

    def arrived(i):
        src, src_cols, dst, dst_cols = sends[i]
        pltpu.make_async_copy(src.at[:, src_cols(me)], dst.at[my_rows, dst_cols], l_in.at[i]).wait()
        wait_bytes(dst.at[pl.ds(0, rows * (n_head - 1)), dst_cols], r_in.at[i])

    def ctx_copy(src, dst, send_sem, recv_sem, device):
        return pltpu.make_async_remote_copy(
            src_ref=src, dst_ref=dst, send_sem=send_sem, recv_sem=recv_sem,
            device_id={"ctx": device}, device_id_type=MESH)

    lane = lax.broadcasted_iota(jnp.int32, (1, HEAD_DIM), 1)
    starts = jnp.full((1, HEAD_DIM), 1 << 20, jnp.int32)
    ends = jnp.full((1, HEAD_DIM), 1 << 20, jnp.int32)
    total = jnp.int32(0)
    for d in range(lens_ref.shape[0]):
        starts = jnp.where(lane == d, total, starts)
        total = total + lens_ref[d]
        ends = jnp.where(lane == d, total, ends)
    row_of = lax.broadcasted_iota(jnp.int32, (piece, HEAD_DIM), 0)
    lane_of = lax.broadcasted_iota(jnp.int32, (piece, HEAD_DIM), 1)
    for r in range(REACH + 1):
        pos = row_of + (ctx - r) * piece
        inside = ((starts <= pos) & (pos < ends)) | ((lane_of == HEAD_DIM - 1) & (pos < 0))
        key_doc[r] = jnp.where(inside, 1.0, 0.0).astype(BF16)
        if r == 0:
            query_doc[...] = jnp.where(inside, 0.0, -FAR).astype(BF16)
    causal = (lax.broadcasted_iota(jnp.int32, (piece, piece), 0)
              <= lax.broadcasted_iota(jnp.int32, (piece, piece), 1))

    def rail_send(r):
        return ctx_copy(kv.at[r], kv.at[r + 2], s_rail.at[r // 2], r_rail.at[r // 2], after)

    def sib_send(k, j):
        return ctx_copy(kv.at[2 * j + 2 * k], kv.at[2 * j + 1], s_sib.at[j], r_sib.at[j], sib)

    def pass_on(r):
        if r < REACH:
            rail_send(r).start()

            @pl.when(core == 0)
            def _():
                sib_send(0, r // 2).start()
        if r > 0:

            @pl.when(core == 1)
            def _():
                sib_send(1, r // 2 - 1).start()

    arrived(0)
    pass_on(0)

    groups = ((1, 2), (3, 4), (5, 6))
    last = len(groups) - 1

    def forward(gi, first_head, heads):
        ra, rb = groups[gi]

        def body(step, carry):
            for u in range(HEADS_STEP):
                j = first_head + step * HEADS_STEP + u
                cols = pl.ds(pl.multiple_of(j * HEAD_DIM, HEAD_DIM), HEAD_DIM)
                query = jnp.concatenate([qb[:, cols], query_doc[...]], axis=1)
                grad = dob[:, cols]

                def both(r):
                    keys = jnp.concatenate([kv[r, :, :HEAD_DIM], key_doc[r]], axis=1)
                    return nt(keys, query), nt(kv[r, :, HEAD_DIM:], grad)

                s_a, dp_a = both(ra)
                s_b, dp_b = both(rb)
                if gi == last:
                    s_0, dp_0 = both(0)
                    s_b = jnp.where(causal, s_0, s_b)
                    dp_b = jnp.where(causal, dp_0, dp_b)
                s = jnp.concatenate([s_a, s_b], axis=0)
                dp = jnp.concatenate([dp_a, dp_b], axis=0)
                top = jnp.max(s, axis=0, keepdims=True)
                p = jnp.exp2(s * TO_EXP2 - top * TO_EXP2)
                probs[gi, j] = p.astype(BF16)
                dprobs[gi, j] = dp
                at = pl.ds(j, 1)
                st_m[gi, at, :] = top * TO_EXP2
                st_l[gi, at, :] = jnp.sum(p, axis=0, keepdims=True)
                st_d[gi, at, :] = jnp.sum(p * dp, axis=0, keepdims=True)
            return carry

        lax.fori_loop(0, heads // HEADS_STEP, body, 0)

    heads_chunk = GROUP_Q // IN_CHUNKS
    for gi in range(len(groups)):
        r = groups[gi][1]
        rail_send(r - 2).wait_recv()
        pass_on(r)
        sib_send(0, gi).wait_recv()
        if gi == 0:
            for chunk in range(IN_CHUNKS):
                arrived(1 + 2 * chunk)
                arrived(2 + 2 * chunk)
                forward(0, chunk * heads_chunk, heads_chunk)
        else:
            forward(gi, 0, GROUP_Q)

    top = jnp.maximum(jnp.maximum(st_m[0], st_m[1]), st_m[2])
    factors = [jnp.exp2(st_m[gi] - top) for gi in range(len(groups))]
    inverse = 1.0 / sum(factors[gi] * st_l[gi] for gi in range(len(groups)))
    row_delta = jnp.zeros_like(inverse)
    for gi in range(len(groups)):
        gain[gi] = factors[gi] * inverse
        row_delta = row_delta + factors[gi] * inverse * st_d[gi]
    delta[...] = row_delta

    def out_send(first, size, peer):
        cols = pl.ds(first if isinstance(first, int) else pl.multiple_of(first, HEAD_DIM), size)
        return pltpu.make_async_remote_copy(
            src_ref=stage.at[pl.ds(pl.multiple_of(peer * rows, rows), rows), cols],
            dst_ref=out_ref.at[:, column(me, first, size)],
            send_sem=s_out, recv_sem=r_out,
            device_id={"head": peer}, device_id_type=MESH)

    def backward(gi, first_step, steps):
        ra, rb = groups[gi]
        final = gi == 0

        def body(step, carry):
            p_all, ds_all, grad_all, query_all = [], [], [], []
            for u in range(HEADS_STEP):
                j = step * HEADS_STEP + u
                cols = pl.ds(pl.multiple_of(j * HEAD_DIM, HEAD_DIM), HEAD_DIM)
                at = pl.ds(j, 1)
                p = probs[gi, j].astype(F32) * gain[gi, at, :]
                ds = p * (dprobs[gi, j] - delta[at, :])
                if gi == last:
                    p_c, ds_c = p[piece:], ds[piece:]
                    p = jnp.concatenate([p[:piece], jnp.where(causal, 0.0, p_c),
                                         jnp.where(causal, p_c, 0.0)], axis=0)
                    ds = jnp.concatenate([ds[:piece], jnp.where(causal, 0.0, ds_c),
                                          jnp.where(causal, ds_c, 0.0)], axis=0)
                    keys = jnp.concatenate([kv[ra, :, :HEAD_DIM], kv[rb, :, :HEAD_DIM],
                                            kv[0, :, :HEAD_DIM]], axis=0)
                else:
                    keys = jnp.concatenate([kv[ra, :, :HEAD_DIM], kv[rb, :, :HEAD_DIM]], axis=0)
                p = p.astype(BF16)
                ds = ds.astype(BF16)
                p_all.append(p)
                ds_all.append(ds)
                grad_all.append(dob[:, cols])
                query_all.append(qb[:, cols])
                grad_query = tn(ds, keys)
                if gi != last:
                    grad_query = grad_query + dq[j]
                if final:
                    stage[:, cols] = (grad_query * SCALE).astype(BF16)
                else:
                    dq[j] = grad_query
            p = jnp.concatenate(p_all, axis=1)
            ds = jnp.concatenate(ds_all, axis=1)
            grad_value = nn(p, jnp.concatenate(grad_all, axis=0))
            grad_key = nn(ds, jnp.concatenate(query_all, axis=0))
            for i in range(2):
                at = pl.ds(i * piece, piece)
                part[i, :, :HEAD_DIM] += grad_key[i * piece:(i + 1) * piece]
                part[i, :, HEAD_DIM:] += grad_value[i * piece:(i + 1) * piece]
            if gi == last:
                home[:, :HEAD_DIM] += grad_key[2 * piece:]
                home[:, HEAD_DIM:] += grad_value[2 * piece:]
            if final:
                first = step * HEADS_STEP * HEAD_DIM
                for peer in peers:
                    out_send(first, HEADS_STEP * HEAD_DIM, peer).start()
            return carry

        lax.fori_loop(first_step, first_step + steps, body, 0)

    def grail(r):
        return ctx_copy(rail_out.at[r // 2 - 1], rail_in.at[r // 2 - 1],
                        s_grail.at[r // 2 - 1], r_grail.at[r // 2 - 1], before)

    def gsib(j):
        return ctx_copy(odd_out.at[j], odd_in.at[j], s_gsib.at[j], r_gsib.at[j], sib)

    def key_scale():
        which = lax.broadcasted_iota(jnp.int32, (1, 2 * HEAD_DIM), 1)
        return jnp.where(which < HEAD_DIM, SCALE, 1.0)

    home[...] = jnp.zeros_like(home)
    for gi in range(last, -1, -1):
        ra, rb = groups[gi]
        j = ra // 2
        part[...] = jnp.zeros_like(part)
        backward(gi, 0, GROUP_Q // HEADS_STEP)
        odd_out[j] = (part[0] * key_scale()).astype(BF16)
        gsib(j).start()
        part[1] = part[1] * key_scale()
        if gi < last:
            grail(rb + 2).wait_recv()
            part[1] += rail_in[rb // 2].astype(F32)

            @pl.when(core == 0)
            def _():
                gsib(j + 1).wait_recv()
                part[1] += odd_in[j + 1].astype(F32)

        @pl.when(core == 1)
        def _():
            gsib(j).wait_recv()
            part[1] += odd_in[j].astype(F32)

        rail_out[rb // 2 - 1] = part[1].astype(BF16)
        grail(rb).start()

    home[...] = home[...] * key_scale()

    @pl.when(core == 0)
    def _():
        gsib(0).wait_recv()
        home[...] += odd_in[0].astype(F32)

    grail(2).wait_recv()
    own = home[...] + rail_in[0].astype(F32)
    stage[:, q_width:] = own.astype(BF16)
    for peer in peers:
        out_send(q_width, 2 * HEAD_DIM, peer).start()
    mine = pltpu.make_async_copy(stage.at[my_rows, :], out_ref.at[:, column(me, 0, width)], l_out)
    mine.start()

    for i, (src, src_cols, dst, dst_cols) in enumerate(sends):
        wait_bytes(dst.at[pl.ds(0, rows * (n_head - 1)), dst_cols], s_in.at[i])
    for j in range(len(groups)):
        rail_send(2 * j).wait_send()
        sib_send(0, j).wait_send()
        gsib(j).wait_send()
        grail(2 * j + 2).wait_send()
    mine.wait()
    wait_bytes(out_ref.at[:, pl.ds(0, width * (n_head - 1))], s_out)
    wait_bytes(out_ref.at[:, pl.ds(0, width * (n_head - 1))], r_out)


def per_device(n_head, n_ctx, merged_qkv, out_grads, doc_lengths):
    rows = merged_qkv.shape[0]
    piece = rows * n_head
    n_groups = REACH // 2
    pair = 2 * HEAD_DIM
    dma = pltpu.SemaphoreType.DMA
    n_in = 1 + 2 * IN_CHUNKS
    macs = 5 * GROUP_Q * piece * (REACH + 1) * piece * HEAD_DIM
    return pl.pallas_call(
        functools.partial(kernel, n_head, n_ctx),
        out_shape=jax.ShapeDtypeStruct(merged_qkv.shape, BF16),
        in_specs=[pl.BlockSpec(memory_space=pltpu.SMEM), pl.BlockSpec(memory_space=pl.ANY),
                  pl.BlockSpec(memory_space=pl.ANY)],
        out_specs=pl.BlockSpec(memory_space=pltpu.VMEM),
        scratch_shapes=[
            pltpu.VMEM((REACH + 1, piece, pair), BF16),
            pltpu.VMEM((REACH + 1, piece, HEAD_DIM), BF16),
            pltpu.VMEM((piece, HEAD_DIM), BF16),
            pltpu.VMEM((piece, GROUP_Q * HEAD_DIM), BF16),
            pltpu.VMEM((piece, GROUP_Q * HEAD_DIM), BF16),
            pltpu.VMEM((n_groups, GROUP_Q, 2 * piece, piece), BF16),
            pltpu.VMEM((n_groups, GROUP_Q, 2 * piece, piece), F32),
            pltpu.VMEM((n_groups, GROUP_Q, piece), F32),
            pltpu.VMEM((n_groups, GROUP_Q, piece), F32),
            pltpu.VMEM((n_groups, GROUP_Q, piece), F32),
            pltpu.VMEM((n_groups, GROUP_Q, piece), F32),
            pltpu.VMEM((GROUP_Q, piece), F32),
            pltpu.VMEM((GROUP_Q, piece, HEAD_DIM), F32),
            pltpu.VMEM((piece, pair), F32),
            pltpu.VMEM((2, piece, pair), F32),
            pltpu.VMEM((n_groups, piece, pair), BF16),
            pltpu.VMEM((n_groups, piece, pair), BF16),
            pltpu.VMEM((n_groups, piece, pair), BF16),
            pltpu.VMEM((n_groups, piece, pair), BF16),
            pltpu.VMEM((piece, (GROUP_Q + 2) * HEAD_DIM), BF16),
            dma((n_in,)), dma((n_in,)), dma((n_in,)),
            dma((n_groups,)), dma((n_groups,)), dma((n_groups,)), dma((n_groups,)),
            dma((n_groups,)), dma((n_groups,)), dma((n_groups,)), dma((n_groups,)),
            dma, dma, dma,
        ],
        compiler_params=pltpu.CompilerParams(
            collective_id=0, has_side_effects=True, vmem_limit_bytes=56 * 1024 * 1024),
        cost_estimate=pl.CostEstimate(
            flops=2 * macs, bytes_accessed=4 * merged_qkv.size * 2,
            transcendentals=GROUP_Q * piece * piece * REACH),
    )(doc_lengths, merged_qkv, out_grads)


def solution(mesh):
    placed = (P(("ctx", "head"), None), P(("ctx", "head"), None), P())
    body = functools.partial(per_device, mesh.shape["head"], mesh.shape["ctx"])
    return jax.shard_map(
        body, mesh=mesh, in_specs=placed, out_specs=P(("ctx", "head"), None), check_vma=False
    )
```

time: 268 us -> 83.5 us (0.31)
  the two profiles are of different devices: /device:TPU:32 before, /device:TPU:1 now
where the time goes in v1:
time: 83.5 us; the launch traced here: 83.3 us
  Pallas kernels  81.3 us (97%)
  local copies, waits for them, and re-layouts  1.97 us (2%)
    pallas_call x1, Pallas kernels, per_device(): pl.pallas_call(functools.partial(kernel, n_head, n_ctx), out_shape=jax.Sh...  81.3 us
    unnamed x1, local copies, waits for them, and re-layouts  1.97 us

profile of v1, /device:TPU:1, one launch (start us, length us, event | category | flops | bytes accessed | tf_op | source)
XLA Modules:
  0.0 83.3 jit_solution(15833306114743819403)
XLA Ops:
  0.0 81.3 %shard_map.37 = bf16[32,10240]{1,0:T(8,128)(2,1)} custom-call(s32[64]{0:T(128)} %lens_ref.1, bf16[32,10240]{1,0:T(8,128)(2,1)} %qkv_ref.1, bf16[32,8192]{1,0:T(8,128)(2,1)} %grads_ref.1), custom_call_target="tpu_custom_call" | custom-call | flops 4697620480 | bytes 2621440 | tf_op jit(solution)/shard_map/pallas_call | solution.py:330
  81.3 2.0 %copy.5 = bf16[32,10240]{1,0:T(8,128)(2,1)} copy(bf16[32,10240]{1,0:T(8,128)(2,1)} %shard_map.37) | data formatting | bytes 1310720

commit v2 on v1

--- a/solution.py
+++ b/solution.py
@@ -16,8 +16,9 @@
 TO_EXP2 = SCALE * math.log2(math.e)
 FAR = 2.0 ** 100
 F32, BF16 = jnp.float32, jnp.bfloat16
-IN_CHUNKS = 2
+IN_CHUNKS = 4
 HEADS_STEP = 2
+Z_CHIPS = 8
 
 
 def nt(a, b):
@@ -38,8 +39,8 @@
 
 def kernel(n_head, n_ctx, lens_ref, qkv_ref, grads_ref, out_ref,
            kv, key_doc, query_doc, qb, dob, probs, dprobs, st_m, st_l, st_d, gain, delta,
-           dq, home, part, odd_out, odd_in, rail_out, rail_in, stage,
-           s_in, r_in, l_in, s_rail, r_rail, s_sib, r_sib, s_grail, r_grail, s_gsib, r_gsib,
+           dq, home, part, even, relay_kv, relay_grads, odd_out, odd_in, rail_out, rail_in, stage,
+           s_in, r_in, l_in, s_rail, r_rail, s_relay, r_relay, s_back, r_back, s_sib, r_sib, s_grail, r_grail, s_gsib, r_gsib,
            s_out, r_out, l_out):
     rows = qkv_ref.shape[0]
     piece = kv.shape[1]
@@ -49,16 +50,36 @@
     ctx = lax.axis_index("ctx")
     core = lax.rem(ctx, 2)
     sib = ctx + 1 - 2 * core
-    after = lax.rem(ctx + 2, n_ctx)
-    before = lax.rem(ctx + n_ctx - 2, n_ctx)
+    z = lax.rem(ctx // 2, Z_CHIPS)
+    odd_row = lax.rem(me, 2) == 1
+    starts_run, ends_run = z == 0, z == Z_CHIPS - 1
+    relays = (odd_row & starts_run) | (jnp.logical_not(odd_row) & ends_run)
+
+    def shifted(steps):
+        return lax.rem(ctx + n_ctx + 2 * steps, n_ctx)
+
+    after = jnp.where(ends_run, jnp.where(odd_row, shifted(1 - Z_CHIPS), shifted(Z_CHIPS)), shifted(1))
+    before = jnp.where(starts_run, jnp.where(odd_row, shifted(-Z_CHIPS), shifted(Z_CHIPS - 1)), shifted(-1))
+    relay_from = jnp.where(odd_row, shifted(Z_CHIPS - 1), shifted(-Z_CHIPS))
+    relay_to = jnp.where(odd_row, shifted(Z_CHIPS), shifted(1 - Z_CHIPS))
     peers = [lax.rem(me + p, n_head) for p in range(1, n_head)]
 
     barrier = pltpu.get_barrier_semaphore()
+
+    def greet(axis, other):
+        pl.semaphore_signal(barrier, inc=1, device_id={axis: other}, device_id_type=MESH)
+
     for peer in peers:
-        pl.semaphore_signal(barrier, inc=1, device_id={"head": peer}, device_id_type=MESH)
+        greet("head", peer)
     for other in (sib, after, before):
-        pl.semaphore_signal(barrier, inc=1, device_id={"ctx": other}, device_id_type=MESH)
-    pl.semaphore_wait(barrier, len(peers) + 3)
+        greet("ctx", other)
+
+    @pl.when(relays)
+    def _():
+        greet("ctx", relay_from)
+        greet("ctx", relay_to)
+
+    pl.semaphore_wait(barrier, jnp.where(relays, len(peers) + 5, len(peers) + 3))
 
     my_rows = pl.ds(pl.multiple_of(me * rows, rows), rows)
 
@@ -69,23 +90,46 @@
         return pl.ds(pl.multiple_of(group * q_width + first, HEAD_DIM), size)
 
     step_w = q_width // IN_CHUNKS
-    sends = [(qkv_ref, lambda g: column(g, q_width, 2 * HEAD_DIM), kv.at[0], pl.ds(0, 2 * HEAD_DIM))]
-    for chunk in range(IN_CHUNKS):
-        cols = pl.ds(chunk * step_w, step_w)
-        sends.append((qkv_ref, lambda g, f=chunk * step_w: column(g, f, step_w), qb, cols))
-        sends.append((grads_ref, lambda g, f=chunk * step_w: grad_column(g, f, step_w), dob, cols))
-    for i, (src, src_cols, dst, dst_cols) in enumerate(sends):
-        for peer in peers:
-            pltpu.make_async_remote_copy(
-                src_ref=src.at[:, src_cols(peer)], dst_ref=dst.at[my_rows, dst_cols],
-                send_sem=s_in.at[i], recv_sem=r_in.at[i],
-                device_id={"head": peer}, device_id_type=MESH).start()
-        pltpu.make_async_copy(src.at[:, src_cols(me)], dst.at[my_rows, dst_cols], l_in.at[i]).start()
-
-    def arrived(i):
-        src, src_cols, dst, dst_cols = sends[i]
-        pltpu.make_async_copy(src.at[:, src_cols(me)], dst.at[my_rows, dst_cols], l_in.at[i]).wait()
-        wait_bytes(dst.at[pl.ds(0, rows * (n_head - 1)), dst_cols], r_in.at[i])
+    others = pl.ds(0, rows * (n_head - 1))
+
+    def sends(chunk):
+        if chunk is None:
+            return [(qkv_ref, lambda g: column(g, q_width, 2 * HEAD_DIM), kv.at[0],
+                     pl.ds(0, 2 * HEAD_DIM), 0)]
+        first = chunk * step_w
+        cols = pl.ds(pl.multiple_of(first, HEAD_DIM), step_w)
+        return [(qkv_ref, lambda g: column(g, first, step_w), qb, cols, 1 + 2 * chunk),
+                (grads_ref, lambda g: grad_column(g, first, step_w), dob, cols, 2 + 2 * chunk)]
+
+    def send_part(chunk):
+        for src, src_cols, dst, dst_cols, i in sends(chunk):
+            for peer in peers:
+                pltpu.make_async_remote_copy(
+                    src_ref=src.at[:, src_cols(peer)], dst_ref=dst.at[my_rows, dst_cols],
+                    send_sem=s_in.at[i], recv_sem=r_in.at[i],
+                    device_id={"head": peer}, device_id_type=MESH).start()
+            pltpu.make_async_copy(
+                src.at[:, src_cols(me)], dst.at[my_rows, dst_cols], l_in.at[i]).start()
+
+    def arrived(chunk):
+        for src, src_cols, dst, dst_cols, i in sends(chunk):
+            pltpu.make_async_copy(
+                src.at[:, src_cols(me)], dst.at[my_rows, dst_cols], l_in.at[i]).wait()
+            wait_bytes(dst.at[others, dst_cols], r_in.at[i])
+
+    def all_sent(chunk):
+        for src, src_cols, dst, dst_cols, i in sends(chunk):
+            wait_bytes(dst.at[others, dst_cols], s_in.at[i])
+
+    def chunks(first, body):
+        def step(chunk, carry):
+            body(chunk)
+            return carry
+
+        lax.fori_loop(first, IN_CHUNKS, step, 0)
+
+    send_part(None)
+    send_part(0)
 
     def ctx_copy(src, dst, send_sem, recv_sem, device):
         return pltpu.make_async_remote_copy(
@@ -114,12 +158,26 @@
     def rail_send(r):
         return ctx_copy(kv.at[r], kv.at[r + 2], s_rail.at[r // 2], r_rail.at[r // 2], after)
 
+    def hand_over(r):
+        return ctx_copy(kv.at[r], relay_kv.at[r // 2], s_rail.at[r // 2], r_relay.at[r // 2], after)
+
+    def relay_send(r):
+        return ctx_copy(relay_kv.at[r // 2], kv.at[r + 2], s_relay.at[r // 2], r_rail.at[r // 2],
+                        relay_to)
+
     def sib_send(k, j):
         return ctx_copy(kv.at[2 * j + 2 * k], kv.at[2 * j + 1], s_sib.at[j], r_sib.at[j], sib)
 
     def pass_on(r):
         if r < REACH:
-            rail_send(r).start()
+
+            @pl.when(ends_run)
+            def _():
+                hand_over(r).start()
+
+            @pl.when(jnp.logical_not(ends_run))
+            def _():
+                rail_send(r).start()
 
             @pl.when(core == 0)
             def _():
@@ -130,8 +188,15 @@
             def _():
                 sib_send(1, r // 2 - 1).start()
 
-    arrived(0)
+    def relay(r):
+        @pl.when(relays)
+        def _():
+            hand_over(r).wait_recv()
+            relay_send(r).start()
+
+    arrived(None)
     pass_on(0)
+    chunks(1, send_part)
 
     groups = ((1, 2), (3, 4), (5, 6))
     last = len(groups) - 1
@@ -146,18 +211,16 @@
                 query = jnp.concatenate([qb[:, cols], query_doc[...]], axis=1)
                 grad = dob[:, cols]
 
-                def both(r):
-                    keys = jnp.concatenate([kv[r, :, :HEAD_DIM], key_doc[r]], axis=1)
-                    return nt(keys, query), nt(kv[r, :, HEAD_DIM:], grad)
-
-                s_a, dp_a = both(ra)
-                s_b, dp_b = both(rb)
+                blocks = (ra, rb, 0) if gi == last else (ra, rb)
+                keys = jnp.concatenate(
+                    [jnp.concatenate([kv[r, :, :HEAD_DIM], key_doc[r]], axis=1) for r in blocks], axis=0)
+                values = jnp.concatenate([kv[r, :, HEAD_DIM:] for r in blocks], axis=0)
+                s = nt(keys, query)
+                dp = nt(values, grad)
                 if gi == last:
-                    s_0, dp_0 = both(0)
-                    s_b = jnp.where(causal, s_0, s_b)
-                    dp_b = jnp.where(causal, dp_0, dp_b)
-                s = jnp.concatenate([s_a, s_b], axis=0)
-                dp = jnp.concatenate([dp_a, dp_b], axis=0)
+                    s, dp = (jnp.concatenate(
+                        [a[:piece], jnp.where(causal, a[2 * piece:], a[piece:2 * piece])], axis=0)
+                        for a in (s, dp))
                 top = jnp.max(s, axis=0, keepdims=True)
                 p = jnp.exp2(s * TO_EXP2 - top * TO_EXP2)
                 probs[gi, j] = p.astype(BF16)
@@ -173,16 +236,20 @@
     heads_chunk = GROUP_Q // IN_CHUNKS
     for gi in range(len(groups)):
         r = groups[gi][1]
+        relay(r - 2)
         rail_send(r - 2).wait_recv()
         pass_on(r)
         sib_send(0, gi).wait_recv()
         if gi == 0:
-            for chunk in range(IN_CHUNKS):
-                arrived(1 + 2 * chunk)
-                arrived(2 + 2 * chunk)
-                forward(0, chunk * heads_chunk, heads_chunk)
-        else:
-            forward(gi, 0, GROUP_Q)
+            arrived(0)
+        forward(gi, 0, heads_chunk)
+
+    def forward_chunk(chunk):
+        arrived(chunk)
+        for gi in range(len(groups)):
+            forward(gi, chunk * heads_chunk, heads_chunk)
+
+    chunks(1, forward_chunk)
 
     top = jnp.maximum(jnp.maximum(st_m[0], st_m[1]), st_m[2])
     factors = [jnp.exp2(st_m[gi] - top) for gi in range(len(groups))]
@@ -201,11 +268,21 @@
             send_sem=s_out, recv_sem=r_out,
             device_id={"head": peer}, device_id_type=MESH)
 
-    def backward(gi, first_step, steps):
+    def backward(gi):
         ra, rb = groups[gi]
         final = gi == 0
 
         def body(step, carry):
+            if gi < last:
+
+                @pl.when(step == 1)
+                def _():
+                    send_sum(gi + 1)
+
+                @pl.when(step == 3)
+                def _():
+                    relay_back(groups[gi + 1][1])
+
             p_all, ds_all, grad_all, query_all = [], [], [], []
             for u in range(HEADS_STEP):
                 j = step * HEADS_STEP + u
@@ -253,11 +330,25 @@
                     out_send(first, HEADS_STEP * HEAD_DIM, peer).start()
             return carry
 
-        lax.fori_loop(first_step, first_step + steps, body, 0)
+        lax.fori_loop(0, GROUP_Q // HEADS_STEP, body, 0)
 
     def grail(r):
-        return ctx_copy(rail_out.at[r // 2 - 1], rail_in.at[r // 2 - 1],
-                        s_grail.at[r // 2 - 1], r_grail.at[r // 2 - 1], before)
+        i = r // 2 - 1
+        return ctx_copy(rail_out.at[i], rail_in.at[i], s_grail.at[i], r_grail.at[i], before)
+
+    def grail_over(r):
+        i = r // 2 - 1
+        return ctx_copy(rail_out.at[i], relay_grads.at[i], s_grail.at[i], r_back.at[i], before)
+
+    def grail_relay(r):
+        i = r // 2 - 1
+        return ctx_copy(relay_grads.at[i], rail_in.at[i], s_back.at[i], r_grail.at[i], relay_from)
+
+    def relay_back(r):
+        @pl.when(relays)
+        def _():
+            grail_over(r).wait_recv()
+            grail_relay(r).start()
 
     def gsib(j):
         return ctx_copy(odd_out.at[j], odd_in.at[j], s_gsib.at[j], r_gsib.at[j], sib)
@@ -266,31 +357,41 @@
         which = lax.broadcasted_iota(jnp.int32, (1, 2 * HEAD_DIM), 1)
         return jnp.where(which < HEAD_DIM, SCALE, 1.0)
 
-    home[...] = jnp.zeros_like(home)
-    for gi in range(last, -1, -1):
-        ra, rb = groups[gi]
-        j = ra // 2
-        part[...] = jnp.zeros_like(part)
-        backward(gi, 0, GROUP_Q // HEADS_STEP)
-        odd_out[j] = (part[0] * key_scale()).astype(BF16)
-        gsib(j).start()
-        part[1] = part[1] * key_scale()
+    def send_sum(gi):
+        rb, j = groups[gi][1], gi
         if gi < last:
             grail(rb + 2).wait_recv()
-            part[1] += rail_in[rb // 2].astype(F32)
+            even[...] += rail_in[rb // 2].astype(F32)
 
             @pl.when(core == 0)
             def _():
                 gsib(j + 1).wait_recv()
-                part[1] += odd_in[j + 1].astype(F32)
+                even[...] += odd_in[j + 1].astype(F32)
 
         @pl.when(core == 1)
         def _():
             gsib(j).wait_recv()
-            part[1] += odd_in[j].astype(F32)
-
-        rail_out[rb // 2 - 1] = part[1].astype(BF16)
-        grail(rb).start()
+            even[...] += odd_in[j].astype(F32)
+
+        rail_out[rb // 2 - 1] = even[...].astype(BF16)
+
+        @pl.when(starts_run)
+        def _():
+            grail_over(rb).start()
+
+        @pl.when(jnp.logical_not(starts_run))
+        def _():
+            grail(rb).start()
+
+    home[...] = jnp.zeros_like(home)
+    for gi in range(last, -1, -1):
+        part[...] = jnp.zeros_like(part)
+        backward(gi)
+        odd_out[gi] = (part[0] * key_scale()).astype(BF16)
+        gsib(gi).start()
+        even[...] = part[1] * key_scale()
+    send_sum(0)
+    relay_back(groups[0][1])
 
     home[...] = home[...] * key_scale()
 
@@ -307,10 +408,16 @@
     mine = pltpu.make_async_copy(stage.at[my_rows, :], out_ref.at[:, column(me, 0, width)], l_out)
     mine.start()
 
-    for i, (src, src_cols, dst, dst_cols) in enumerate(sends):
-        wait_bytes(dst.at[pl.ds(0, rows * (n_head - 1)), dst_cols], s_in.at[i])
+    all_sent(None)
+    chunks(0, all_sent)
     for j in range(len(groups)):
         rail_send(2 * j).wait_send()
+
+        @pl.when(relays)
+        def _():
+            relay_send(2 * j).wait_send()
+            grail_relay(2 * j + 2).wait_send()
+
         sib_send(0, j).wait_send()
         gsib(j).wait_send()
         grail(2 * j + 2).wait_send()
@@ -349,6 +456,9 @@
             pltpu.VMEM((GROUP_Q, piece, HEAD_DIM), F32),
             pltpu.VMEM((piece, pair), F32),
             pltpu.VMEM((2, piece, pair), F32),
+            pltpu.VMEM((piece, pair), F32),
+            pltpu.VMEM((n_groups, piece, pair), BF16),
+            pltpu.VMEM((n_groups, piece, pair), BF16),
             pltpu.VMEM((n_groups, piece, pair), BF16),
             pltpu.VMEM((n_groups, piece, pair), BF16),
             pltpu.VMEM((n_groups, piece, pair), BF16),
@@ -356,7 +466,9 @@
             pltpu.VMEM((piece, (GROUP_Q + 2) * HEAD_DIM), BF16),
             dma((n_in,)), dma((n_in,)), dma((n_in,)),
             dma((n_groups,)), dma((n_groups,)), dma((n_groups,)), dma((n_groups,)),
+            dma((n_groups,)), dma((n_groups,)),
             dma((n_groups,)), dma((n_groups,)), dma((n_groups,)), dma((n_groups,)),
+            dma((n_groups,)), dma((n_groups,)),
             dma, dma, dma,
         ],
         compiler_params=pltpu.CompilerParams(

time: 83.5 us -> 82.8 us (level)
  Pallas kernels: 81.3 us -> 80 us
    pallas_call x1, Pallas kernels: 81.3 us -> 80 us  [per_device(): pl.pallas_call(functools.partial(kernel, n_head, n_ctx), out_shape=jax.Sh...]
where the time goes in v2:
time: 82.8 us; the launch traced here: 82 us
  Pallas kernels  80 us (97%)
  local copies, waits for them, and re-layouts  1.97 us (2%)
    pallas_call x1, Pallas kernels, per_device(): pl.pallas_call(functools.partial(kernel, n_head, n_ctx), out_shape=jax.Sh...  80 us
    unnamed x1, local copies, waits for them, and re-layouts  1.97 us

profile of v2, /device:TPU:1, one launch (start us, length us, event | category | flops | bytes accessed | tf_op | source)
XLA Modules:
  0.0 82.0 jit_solution(15428944674764316958)
XLA Ops:
  0.0 80.0 %shard_map.37 = bf16[32,10240]{1,0:T(8,128)(2,1)} custom-call(s32[64]{0:T(128)} %lens_ref.1, bf16[32,10240]{1,0:T(8,128)(2,1)} %qkv_ref.1, bf16[32,8192]{1,0:T(8,128)(2,1)} %grads_ref.1), custom_call_target="tpu_custom_call" | custom-call | flops 4697620480 | bytes 2621440 | tf_op jit(solution)/shard_map/pallas_call | solution.py:437
  80.0 2.0 %copy.5 = bf16[32,10240]{1,0:T(8,128)(2,1)} copy(bf16[32,10240]{1,0:T(8,128)(2,1)} %shard_map.37) | data formatting | bytes 1310720

commit v3 on v2

--- a/solution.py
+++ b/solution.py
@@ -129,7 +129,6 @@
         lax.fori_loop(first, IN_CHUNKS, step, 0)
 
     send_part(None)
-    send_part(0)
 
     def ctx_copy(src, dst, send_sem, recv_sem, device):
         return pltpu.make_async_remote_copy(
@@ -196,7 +195,7 @@
 
     arrived(None)
     pass_on(0)
-    chunks(1, send_part)
+    send_part(0)
 
     groups = ((1, 2), (3, 4), (5, 6))
     last = len(groups) - 1
@@ -237,12 +236,19 @@
     for gi in range(len(groups)):
         r = groups[gi][1]
         relay(r - 2)
+        if gi == last:
+            arrived(0)
+            for g in range(last):
+                sib_send(0, g).wait_recv()
+                forward(g, 0, heads_chunk)
         rail_send(r - 2).wait_recv()
         pass_on(r)
-        sib_send(0, gi).wait_recv()
         if gi == 0:
-            arrived(0)
-        forward(gi, 0, heads_chunk)
+            send_part(1)
+        elif gi == 1:
+            chunks(2, send_part)
+    sib_send(0, last).wait_recv()
+    forward(last, 0, heads_chunk)
 
     def forward_chunk(chunk):
         arrived(chunk)
@@ -277,11 +283,10 @@
 
                 @pl.when(step == 1)
                 def _():
+                    if final:
+                        relay_back(groups[last][1])
                     send_sum(gi + 1)
 
-                @pl.when(step == 3)
-                def _():
-                    relay_back(groups[gi + 1][1])
 
             p_all, ds_all, grad_all, query_all = [], [], [], []
             for u in range(HEADS_STEP):
@@ -390,6 +395,7 @@
         odd_out[gi] = (part[0] * key_scale()).astype(BF16)
         gsib(gi).start()
         even[...] = part[1] * key_scale()
+    relay_back(groups[1][1])
     send_sum(0)
     relay_back(groups[0][1])
 

time: 82.8 us -> 77.5 us (0.936)
  Pallas kernels: 80 us -> 75.3 us
    pallas_call x1, Pallas kernels: 80 us -> 75.3 us  [per_device(): pl.pallas_call(functools.partial(kernel, n_head, n_ctx), out_shape=jax.Sh...]
where the time goes in v3:
time: 77.5 us; the launch traced here: 77.3 us
  Pallas kernels  75.3 us (97%)
  local copies, waits for them, and re-layouts  1.97 us (3%)
    pallas_call x1, Pallas kernels, per_device(): pl.pallas_call(functools.partial(kernel, n_head, n_ctx), out_shape=jax.Sh...  75.3 us
    unnamed x1, local copies, waits for them, and re-layouts  1.97 us

profile of v3, /device:TPU:1, one launch (start us, length us, event | category | flops | bytes accessed | tf_op | source)
XLA Modules:
  0.0 77.3 jit_solution(16197093183924549825)
XLA Ops:
  0.0 75.3 %shard_map.37 = bf16[32,10240]{1,0:T(8,128)(2,1)} custom-call(s32[64]{0:T(128)} %lens_ref.1, bf16[32,10240]{1,0:T(8,128)(2,1)} %qkv_ref.1, bf16[32,8192]{1,0:T(8,128)(2,1)} %grads_ref.1), custom_call_target="tpu_custom_call" | custom-call | flops 4697620480 | bytes 2621440 | tf_op jit(solution)/shard_map/pallas_call | solution.py:443
  75.3 2.0 %copy.5 = bf16[32,10240]{1,0:T(8,128)(2,1)} copy(bf16[32,10240]{1,0:T(8,128)(2,1)} %shard_map.37) | data formatting | bytes 1310720

commit v4 on v3

--- a/solution.py
+++ b/solution.py
@@ -29,19 +29,16 @@
     return lax.dot_general(a, b, (((1,), (0,)), ((), ())), preferred_element_type=F32)
 
 
-def tn(a, b):
-    return lax.dot_general(a, b, (((0,), (0,)), ((), ())), preferred_element_type=F32)
-
-
 def wait_bytes(ref, sem):
     pltpu.make_async_copy(ref, ref, sem).wait()
 
 
 def kernel(n_head, n_ctx, lens_ref, qkv_ref, grads_ref, out_ref,
            kv, key_doc, query_doc, qb, dob, probs, dprobs, st_m, st_l, st_d, gain, delta,
-           dq, home, part, even, relay_kv, relay_grads, odd_out, odd_in, rail_out, rail_in, stage,
-           s_in, r_in, l_in, s_rail, r_rail, s_relay, r_relay, s_back, r_back, s_sib, r_sib, s_grail, r_grail, s_gsib, r_gsib,
-           s_out, r_out, l_out):
+           key_t, dq, home, part, even, relay_kv, relay_grads, cross_in,
+           odd_out, odd_in, rail_out, rail_in, stage,
+           s_in, r_in, l_in, s_rail, r_rail, s_cross, r_cross, r_back, s_sib, r_sib,
+           s_grail, r_grail, s_gsib, r_gsib, s_out, r_out, l_out):
     rows = qkv_ref.shape[0]
     piece = kv.shape[1]
     width = (GROUP_Q + 2) * HEAD_DIM
@@ -51,17 +48,17 @@
     core = lax.rem(ctx, 2)
     sib = ctx + 1 - 2 * core
     z = lax.rem(ctx // 2, Z_CHIPS)
-    odd_row = lax.rem(me, 2) == 1
+    n_groups = REACH // 2
     starts_run, ends_run = z == 0, z == Z_CHIPS - 1
-    relays = (odd_row & starts_run) | (jnp.logical_not(odd_row) & ends_run)
+    crosses = z >= Z_CHIPS - n_groups
 
     def shifted(steps):
         return lax.rem(ctx + n_ctx + 2 * steps, n_ctx)
 
-    after = jnp.where(ends_run, jnp.where(odd_row, shifted(1 - Z_CHIPS), shifted(Z_CHIPS)), shifted(1))
-    before = jnp.where(starts_run, jnp.where(odd_row, shifted(-Z_CHIPS), shifted(Z_CHIPS - 1)), shifted(-1))
-    relay_from = jnp.where(odd_row, shifted(Z_CHIPS - 1), shifted(-Z_CHIPS))
-    relay_to = jnp.where(odd_row, shifted(Z_CHIPS), shifted(1 - Z_CHIPS))
+    after, before = shifted(1), shifted(-1)
+    next_run, last_run = shifted(Z_CHIPS), shifted(-Z_CHIPS)
+    run_start = shifted(-z)
+    run_ends = [shifted(Z_CHIPS - 1 - i) for i in range(n_groups)]
     peers = [lax.rem(me + p, n_head) for p in range(1, n_head)]
 
     barrier = pltpu.get_barrier_semaphore()
@@ -71,15 +68,26 @@
 
     for peer in peers:
         greet("head", peer)
-    for other in (sib, after, before):
-        greet("ctx", other)
-
-    @pl.when(relays)
+    greet("ctx", sib)
+
+    def where(condition, body):
+        pl.when(condition)(body)
+
+    where(jnp.logical_not(starts_run), lambda: greet("ctx", before))
+    where(jnp.logical_not(ends_run), lambda: greet("ctx", after))
+
+    @pl.when(crosses)
     def _():
-        greet("ctx", relay_from)
-        greet("ctx", relay_to)
-
-    pl.semaphore_wait(barrier, jnp.where(relays, len(peers) + 5, len(peers) + 3))
+        for other in (next_run, last_run, run_start):
+            greet("ctx", other)
+
+    @pl.when(starts_run)
+    def _():
+        for other in run_ends:
+            greet("ctx", other)
+
+    greeted = len(peers) + 3 + jnp.where(starts_run, n_groups - 1, 0)
+    pl.semaphore_wait(barrier, greeted + jnp.where(ends_run, 2, jnp.where(crosses, 3, 0)))
 
     my_rows = pl.ds(pl.multiple_of(me * rows, rows), rows)
 
@@ -157,22 +165,18 @@
     def rail_send(r):
         return ctx_copy(kv.at[r], kv.at[r + 2], s_rail.at[r // 2], r_rail.at[r // 2], after)
 
-    def hand_over(r):
-        return ctx_copy(kv.at[r], relay_kv.at[r // 2], s_rail.at[r // 2], r_relay.at[r // 2], after)
-
-    def relay_send(r):
-        return ctx_copy(relay_kv.at[r // 2], kv.at[r + 2], s_relay.at[r // 2], r_rail.at[r // 2],
-                        relay_to)
+    def cross_send():
+        return ctx_copy(kv.at[0], relay_kv, s_cross.at[0], r_cross.at[0], next_run)
+
+    def cross_on():
+        i = Z_CHIPS - 1 - z
+        return ctx_copy(relay_kv, kv.at[2 * i + 2], s_cross.at[1], r_rail.at[i], run_start)
 
     def sib_send(k, j):
         return ctx_copy(kv.at[2 * j + 2 * k], kv.at[2 * j + 1], s_sib.at[j], r_sib.at[j], sib)
 
     def pass_on(r):
         if r < REACH:
-
-            @pl.when(ends_run)
-            def _():
-                hand_over(r).start()
 
             @pl.when(jnp.logical_not(ends_run))
             def _():
@@ -187,73 +191,70 @@
             def _():
                 sib_send(1, r // 2 - 1).start()
 
-    def relay(r):
-        @pl.when(relays)
-        def _():
-            hand_over(r).wait_recv()
-            relay_send(r).start()
-
     arrived(None)
+    where(crosses, lambda: cross_send().start())
     pass_on(0)
     send_part(0)
 
     groups = ((1, 2), (3, 4), (5, 6))
     last = len(groups) - 1
 
-    def forward(gi, first_head, heads):
+    heads_chunk = GROUP_Q // IN_CHUNKS
+
+    def forward(gi, first_head):
         ra, rb = groups[gi]
 
-        def body(step, carry):
-            for u in range(HEADS_STEP):
-                j = first_head + step * HEADS_STEP + u
-                cols = pl.ds(pl.multiple_of(j * HEAD_DIM, HEAD_DIM), HEAD_DIM)
-                query = jnp.concatenate([qb[:, cols], query_doc[...]], axis=1)
-                grad = dob[:, cols]
-
-                blocks = (ra, rb, 0) if gi == last else (ra, rb)
-                keys = jnp.concatenate(
-                    [jnp.concatenate([kv[r, :, :HEAD_DIM], key_doc[r]], axis=1) for r in blocks], axis=0)
-                values = jnp.concatenate([kv[r, :, HEAD_DIM:] for r in blocks], axis=0)
-                s = nt(keys, query)
-                dp = nt(values, grad)
-                if gi == last:
-                    s, dp = (jnp.concatenate(
-                        [a[:piece], jnp.where(causal, a[2 * piece:], a[piece:2 * piece])], axis=0)
-                        for a in (s, dp))
-                top = jnp.max(s, axis=0, keepdims=True)
-                p = jnp.exp2(s * TO_EXP2 - top * TO_EXP2)
-                probs[gi, j] = p.astype(BF16)
-                dprobs[gi, j] = dp
-                at = pl.ds(j, 1)
-                st_m[gi, at, :] = top * TO_EXP2
-                st_l[gi, at, :] = jnp.sum(p, axis=0, keepdims=True)
-                st_d[gi, at, :] = jnp.sum(p * dp, axis=0, keepdims=True)
-            return carry
-
-        lax.fori_loop(0, heads // HEADS_STEP, body, 0)
-
-    heads_chunk = GROUP_Q // IN_CHUNKS
+        for u in range(heads_chunk):
+            j = first_head + u
+            cols = pl.ds(pl.multiple_of(j * HEAD_DIM, HEAD_DIM), HEAD_DIM)
+            query = jnp.concatenate([qb[:, cols], query_doc[...]], axis=1)
+            grad = dob[:, cols]
+
+            blocks = (ra, rb, 0) if gi == last else (ra, rb)
+            keys = jnp.concatenate(
+                [jnp.concatenate([kv[r, :, :HEAD_DIM], key_doc[r]], axis=1) for r in blocks], axis=0)
+            values = jnp.concatenate([kv[r, :, HEAD_DIM:] for r in blocks], axis=0)
+            s = nt(keys, query)
+            dp = nt(values, grad)
+            if gi == last:
+                s, dp = (jnp.concatenate(
+                    [a[:piece], jnp.where(causal, a[2 * piece:], a[piece:2 * piece])], axis=0)
+                    for a in (s, dp))
+            top = jnp.max(s, axis=0, keepdims=True)
+            p = jnp.exp2(s * TO_EXP2 - top * TO_EXP2)
+            probs[gi, j] = p.astype(BF16)
+            dprobs[gi, j] = dp
+            at = pl.ds(j, 1)
+            st_m[gi, at, :] = top * TO_EXP2
+            st_l[gi, at, :] = jnp.sum(p, axis=0, keepdims=True)
+            st_d[gi, at, :] = jnp.sum(p * dp, axis=0, keepdims=True)
+
     for gi in range(len(groups)):
         r = groups[gi][1]
-        relay(r - 2)
         if gi == last:
             arrived(0)
             for g in range(last):
                 sib_send(0, g).wait_recv()
-                forward(g, 0, heads_chunk)
+                forward(g, 0)
         rail_send(r - 2).wait_recv()
         pass_on(r)
         if gi == 0:
             send_part(1)
+
+            @pl.when(crosses)
+            def _():
+                cross_send().wait_recv()
+                cross_on().start()
+
         elif gi == 1:
             chunks(2, send_part)
     sib_send(0, last).wait_recv()
-    forward(last, 0, heads_chunk)
+    forward(last, 0)
 
     def forward_chunk(chunk):
         arrived(chunk)
         for gi in range(len(groups)):
-            forward(gi, chunk * heads_chunk, heads_chunk)
+            forward(gi, chunk * heads_chunk)
 
     chunks(1, forward_chunk)
 
@@ -277,6 +278,7 @@
     def backward(gi):
         ra, rb = groups[gi]
         final = gi == 0
+        heads_step = HEADS_STEP if final else 2 * HEADS_STEP
 
         def body(step, carry):
             if gi < last:
@@ -284,13 +286,14 @@
                 @pl.when(step == 1)
                 def _():
                     if final:
-                        relay_back(groups[last][1])
+                        cross_back(last)
                     send_sum(gi + 1)
 
-
+            blocks = (ra, rb, 0) if gi == last else (ra, rb)
+            keys_t = jnp.concatenate([key_t[r] for r in blocks], axis=1)
             p_all, ds_all, grad_all, query_all = [], [], [], []
-            for u in range(HEADS_STEP):
-                j = step * HEADS_STEP + u
+            for u in range(heads_step):
+                j = step * heads_step + u
                 cols = pl.ds(pl.multiple_of(j * HEAD_DIM, HEAD_DIM), HEAD_DIM)
                 at = pl.ds(j, 1)
                 p = probs[gi, j].astype(F32) * gain[gi, at, :]
@@ -301,21 +304,17 @@
                                          jnp.where(causal, p_c, 0.0)], axis=0)
                     ds = jnp.concatenate([ds[:piece], jnp.where(causal, 0.0, ds_c),
                                           jnp.where(causal, ds_c, 0.0)], axis=0)
-                    keys = jnp.concatenate([kv[ra, :, :HEAD_DIM], kv[rb, :, :HEAD_DIM],
-                                            kv[0, :, :HEAD_DIM]], axis=0)
-                else:
-                    keys = jnp.concatenate([kv[ra, :, :HEAD_DIM], kv[rb, :, :HEAD_DIM]], axis=0)
                 p = p.astype(BF16)
                 ds = ds.astype(BF16)
                 p_all.append(p)
                 ds_all.append(ds)
                 grad_all.append(dob[:, cols])
                 query_all.append(qb[:, cols])
-                grad_query = tn(ds, keys)
+                grad_query = nn(keys_t, ds)
                 if gi != last:
                     grad_query = grad_query + dq[j]
                 if final:
-                    stage[:, cols] = (grad_query * SCALE).astype(BF16)
+                    stage[:, cols] = jnp.transpose(grad_query * SCALE).astype(BF16)
                 else:
                     dq[j] = grad_query
             p = jnp.concatenate(p_all, axis=1)
@@ -335,25 +334,23 @@
                     out_send(first, HEADS_STEP * HEAD_DIM, peer).start()
             return carry
 
-        lax.fori_loop(0, GROUP_Q // HEADS_STEP, body, 0)
+        lax.fori_loop(0, GROUP_Q // heads_step, body, 0)
 
     def grail(r):
         i = r // 2 - 1
         return ctx_copy(rail_out.at[i], rail_in.at[i], s_grail.at[i], r_grail.at[i], before)
 
-    def grail_over(r):
-        i = r // 2 - 1
-        return ctx_copy(rail_out.at[i], relay_grads.at[i], s_grail.at[i], r_back.at[i], before)
-
-    def grail_relay(r):
-        i = r // 2 - 1
-        return ctx_copy(relay_grads.at[i], rail_in.at[i], s_back.at[i], r_grail.at[i], relay_from)
-
-    def relay_back(r):
-        @pl.when(relays)
+    def grail_over(gi):
+        return ctx_copy(rail_out.at[gi], relay_grads, s_grail.at[gi], r_back.at[0], run_ends[gi])
+
+    def grail_home():
+        return ctx_copy(relay_grads, cross_in, s_cross.at[2], r_back.at[1], last_run)
+
+    def cross_back(gi):
+        @pl.when(z == Z_CHIPS - 1 - gi)
         def _():
-            grail_over(r).wait_recv()
-            grail_relay(r).start()
+            grail_over(gi).wait_recv()
+            grail_home().start()
 
     def gsib(j):
         return ctx_copy(odd_out.at[j], odd_in.at[j], s_gsib.at[j], r_gsib.at[j], sib)
@@ -365,8 +362,10 @@
     def send_sum(gi):
         rb, j = groups[gi][1], gi
         if gi < last:
-            grail(rb + 2).wait_recv()
-            even[...] += rail_in[rb // 2].astype(F32)
+            @pl.when(jnp.logical_not(ends_run))
+            def _():
+                grail(rb + 2).wait_recv()
+                even[...] += rail_in[rb // 2].astype(F32)
 
             @pl.when(core == 0)
             def _():
@@ -382,12 +381,14 @@
 
         @pl.when(starts_run)
         def _():
-            grail_over(rb).start()
+            grail_over(gi).start()
 
         @pl.when(jnp.logical_not(starts_run))
         def _():
             grail(rb).start()
 
+    for r in range(REACH + 1):
+        key_t[r] = jnp.transpose(kv[r, :, :HEAD_DIM])
     home[...] = jnp.zeros_like(home)
     for gi in range(last, -1, -1):
         part[...] = jnp.zeros_like(part)
@@ -395,9 +396,9 @@
         odd_out[gi] = (part[0] * key_scale()).astype(BF16)
         gsib(gi).start()
         even[...] = part[1] * key_scale()
-    relay_back(groups[1][1])
+    cross_back(1)
     send_sum(0)
-    relay_back(groups[0][1])
+    cross_back(0)
 
     home[...] = home[...] * key_scale()
 
@@ -406,8 +407,17 @@
         gsib(0).wait_recv()
         home[...] += odd_in[0].astype(F32)
 
-    grail(2).wait_recv()
-    own = home[...] + rail_in[0].astype(F32)
+    @pl.when(jnp.logical_not(ends_run))
+    def _():
+        grail(2).wait_recv()
+        home[...] += rail_in[0].astype(F32)
+
+    @pl.when(crosses)
+    def _():
+        grail_home().wait_recv()
+        home[...] += cross_in[...].astype(F32)
+
+    own = home[...]
     stage[:, q_width:] = own.astype(BF16)
     for peer in peers:
         out_send(q_width, 2 * HEAD_DIM, peer).start()
@@ -417,16 +427,17 @@
     all_sent(None)
     chunks(0, all_sent)
     for j in range(len(groups)):
-        rail_send(2 * j).wait_send()
-
-        @pl.when(relays)
-        def _():
-            relay_send(2 * j).wait_send()
-            grail_relay(2 * j + 2).wait_send()
-
+        where(jnp.logical_not(ends_run), lambda j=j: rail_send(2 * j).wait_send())
         sib_send(0, j).wait_send()
         gsib(j).wait_send()
         grail(2 * j + 2).wait_send()
+
+    @pl.when(crosses)
+    def _():
+        cross_send().wait_send()
+        cross_on().wait_send()
+        grail_home().wait_send()
+
     mine.wait()
     wait_bytes(out_ref.at[:, pl.ds(0, width * (n_head - 1))], s_out)
     wait_bytes(out_ref.at[:, pl.ds(0, width * (n_head - 1))], r_out)
@@ -459,21 +470,23 @@
             pltpu.VMEM((n_groups, GROUP_Q, piece), F32),
             pltpu.VMEM((n_groups, GROUP_Q, piece), F32),
             pltpu.VMEM((GROUP_Q, piece), F32),
-            pltpu.VMEM((GROUP_Q, piece, HEAD_DIM), F32),
+            pltpu.VMEM((REACH + 1, HEAD_DIM, piece), BF16),
+            pltpu.VMEM((GROUP_Q, HEAD_DIM, piece), F32),
             pltpu.VMEM((piece, pair), F32),
             pltpu.VMEM((2, piece, pair), F32),
             pltpu.VMEM((piece, pair), F32),
-            pltpu.VMEM((n_groups, piece, pair), BF16),
-            pltpu.VMEM((n_groups, piece, pair), BF16),
+            pltpu.VMEM((piece, pair), BF16),
+            pltpu.VMEM((piece, pair), BF16),
+            pltpu.VMEM((piece, pair), BF16),
             pltpu.VMEM((n_groups, piece, pair), BF16),
             pltpu.VMEM((n_groups, piece, pair), BF16),
             pltpu.VMEM((n_groups, piece, pair), BF16),
             pltpu.VMEM((n_groups, piece, pair), BF16),
             pltpu.VMEM((piece, (GROUP_Q + 2) * HEAD_DIM), BF16),
             dma((n_in,)), dma((n_in,)), dma((n_in,)),
-            dma((n_groups,)), dma((n_groups,)), dma((n_groups,)), dma((n_groups,)),
+            dma((n_groups,)), dma((n_groups,)), dma((3,)), dma((1,)), dma((2,)),
             dma((n_groups,)), dma((n_groups,)),
-            dma((n_groups,)), dma((n_groups,)), dma((n_groups,)), dma((n_groups,)),
+            dma((n_groups,)), dma((n_groups,)),
             dma((n_groups,)), dma((n_groups,)),
             dma, dma, dma,
         ],

time: 77.5 us -> 76.2 us (0.983)
  Pallas kernels: 75.3 us -> 74 us
    pallas_call x1, Pallas kernels: 75.3 us -> 74 us  [per_device(): pl.pallas_call(functools.partial(kernel, n_head, n_ctx), out_shape=jax.Sh...]
where the time goes in v4:
time: 76.2 us; the launch traced here: 76 us
  Pallas kernels  74 us (97%)
  local copies, waits for them, and re-layouts  1.97 us (3%)
    pallas_call x1, Pallas kernels, per_device(): pl.pallas_call(functools.partial(kernel, n_head, n_ctx), out_shape=jax.Sh...  74 us
    unnamed x1, local copies, waits for them, and re-layouts  1.97 us

profile of v4, /device:TPU:1, one launch (start us, length us, event | category | flops | bytes accessed | tf_op | source)
XLA Modules:
  0.0 76.0 jit_solution(487974032981312586)
XLA Ops:
  0.0 74.0 %shard_map.37 = bf16[32,10240]{1,0:T(8,128)(2,1)} custom-call(s32[64]{0:T(128)} %lens_ref.1, bf16[32,10240]{1,0:T(8,128)(2,1)} %qkv_ref.1, bf16[32,8192]{1,0:T(8,128)(2,1)} %grads_ref.1), custom_call_target="tpu_custom_call" | custom-call | flops 4697620480 | bytes 2621440 | tf_op jit(solution)/shard_map/pallas_call | solution.py:454
  74.0 2.0 %copy.5 = bf16[32,10240]{1,0:T(8,128)(2,1)} copy(bf16[32,10240]{1,0:T(8,128)(2,1)} %shard_map.37) | data formatting | bytes 1310720

commit v5 on v4

--- a/solution.py
+++ b/solution.py
@@ -29,13 +29,17 @@
     return lax.dot_general(a, b, (((1,), (0,)), ((), ())), preferred_element_type=F32)
 
 
+def tn(a, b):
+    return lax.dot_general(a, b, (((0,), (0,)), ((), ())), preferred_element_type=F32)
+
+
 def wait_bytes(ref, sem):
     pltpu.make_async_copy(ref, ref, sem).wait()
 
 
 def kernel(n_head, n_ctx, lens_ref, qkv_ref, grads_ref, out_ref,
            kv, key_doc, query_doc, qb, dob, probs, dprobs, st_m, st_l, st_d, gain, delta,
-           key_t, dq, home, part, even, relay_kv, relay_grads, cross_in,
+           dq, home, part, even, relay_kv, relay_grads, cross_in,
            odd_out, odd_in, rail_out, rail_in, stage,
            s_in, r_in, l_in, s_rail, r_rail, s_cross, r_cross, r_back, s_sib, r_sib,
            s_grail, r_grail, s_gsib, r_gsib, s_out, r_out, l_out):
@@ -71,7 +75,9 @@
     greet("ctx", sib)
 
     def where(condition, body):
-        pl.when(condition)(body)
+        @pl.when(condition)
+        def _():
+            body()
 
     where(jnp.logical_not(starts_run), lambda: greet("ctx", before))
     where(jnp.logical_not(ends_run), lambda: greet("ctx", after))
@@ -109,15 +115,26 @@
         return [(qkv_ref, lambda g: column(g, first, step_w), qb, cols, 1 + 2 * chunk),
                 (grads_ref, lambda g: grad_column(g, first, step_w), dob, cols, 2 + 2 * chunk)]
 
-    def send_part(chunk):
+    def send_to(chunk, targets):
         for src, src_cols, dst, dst_cols, i in sends(chunk):
-            for peer in peers:
+            for peer in targets:
                 pltpu.make_async_remote_copy(
                     src_ref=src.at[:, src_cols(peer)], dst_ref=dst.at[my_rows, dst_cols],
                     send_sem=s_in.at[i], recv_sem=r_in.at[i],
                     device_id={"head": peer}, device_id_type=MESH).start()
+
+    def send_along_x(chunk):
+        for src, src_cols, dst, dst_cols, i in sends(chunk):
             pltpu.make_async_copy(
                 src.at[:, src_cols(me)], dst.at[my_rows, dst_cols], l_in.at[i]).start()
+        send_to(chunk, peers[1::2])
+
+    def send_across_y(chunk):
+        send_to(chunk, peers[0::2])
+
+    def send_all(chunk):
+        send_along_x(chunk)
+        send_across_y(chunk)
 
     def arrived(chunk):
         for src, src_cols, dst, dst_cols, i in sends(chunk):
@@ -129,14 +146,14 @@
         for src, src_cols, dst, dst_cols, i in sends(chunk):
             wait_bytes(dst.at[others, dst_cols], s_in.at[i])
 
-    def chunks(first, body):
+    def chunks(first, end, body):
         def step(chunk, carry):
             body(chunk)
             return carry
 
-        lax.fori_loop(first, IN_CHUNKS, step, 0)
-
-    send_part(None)
+        lax.fori_loop(first, end, step, 0)
+
+    send_all(None)
 
     def ctx_copy(src, dst, send_sem, recv_sem, device):
         return pltpu.make_async_remote_copy(
@@ -162,39 +179,46 @@
     causal = (lax.broadcasted_iota(jnp.int32, (piece, piece), 0)
               <= lax.broadcasted_iota(jnp.int32, (piece, piece), 1))
 
-    def rail_send(r):
-        return ctx_copy(kv.at[r], kv.at[r + 2], s_rail.at[r // 2], r_rail.at[r // 2], after)
-
-    def cross_send():
-        return ctx_copy(kv.at[0], relay_kv, s_cross.at[0], r_cross.at[0], next_run)
-
-    def cross_on():
-        i = Z_CHIPS - 1 - z
-        return ctx_copy(relay_kv, kv.at[2 * i + 2], s_cross.at[1], r_rail.at[i], run_start)
+    def half(part_no):
+        return pl.ds(part_no * (piece // 2), piece // 2)
+
+    def rail_send(r, part_no):
+        at, i = half(part_no), r // 2
+        return ctx_copy(kv.at[r, at], kv.at[r + 2, at], s_rail.at[i, part_no], r_rail.at[i, part_no], after)
+
+    def cross_send(part_no):
+        at = half(part_no)
+        return ctx_copy(kv.at[0, at], relay_kv.at[at], s_cross.at[part_no], r_cross.at[part_no], next_run)
+
+    def cross_on(part_no):
+        i, at = Z_CHIPS - 1 - z, half(part_no)
+        return ctx_copy(relay_kv.at[at], kv.at[2 * i + 2, at], s_cross.at[2 + part_no],
+                        r_rail.at[i, part_no], run_start)
 
     def sib_send(k, j):
         return ctx_copy(kv.at[2 * j + 2 * k], kv.at[2 * j + 1], s_sib.at[j], r_sib.at[j], sib)
 
     def pass_on(r):
+        for part_no in range(2):
+            if r > 0:
+                rail_send(r - 2, part_no).wait_recv()
+            if r < REACH:
+                where(jnp.logical_not(ends_run), lambda: rail_send(r, part_no).start())
         if r < REACH:
-
-            @pl.when(jnp.logical_not(ends_run))
-            def _():
-                rail_send(r).start()
-
-            @pl.when(core == 0)
-            def _():
-                sib_send(0, r // 2).start()
+            where(core == 0, lambda: sib_send(0, r // 2).start())
         if r > 0:
-
-            @pl.when(core == 1)
-            def _():
-                sib_send(1, r // 2 - 1).start()
+            where(core == 1, lambda: sib_send(1, r // 2 - 1).start())
 
     arrived(None)
-    where(crosses, lambda: cross_send().start())
+
+    @pl.when(crosses)
+    def _():
+        for part_no in range(2):
+            cross_send(part_no).start()
+
     pass_on(0)
-    send_part(0)
+    chunks(0, IN_CHUNKS, send_along_x)
+    where(jnp.logical_not(crosses), lambda: chunks(0, IN_CHUNKS, send_across_y))
 
     groups = ((1, 2), (3, 4), (5, 6))
     last = len(groups) - 1
@@ -229,34 +253,28 @@
             st_l[gi, at, :] = jnp.sum(p, axis=0, keepdims=True)
             st_d[gi, at, :] = jnp.sum(p * dp, axis=0, keepdims=True)
 
-    for gi in range(len(groups)):
-        r = groups[gi][1]
-        if gi == last:
-            arrived(0)
-            for g in range(last):
-                sib_send(0, g).wait_recv()
-                forward(g, 0)
-        rail_send(r - 2).wait_recv()
-        pass_on(r)
-        if gi == 0:
-            send_part(1)
-
-            @pl.when(crosses)
-            def _():
-                cross_send().wait_recv()
-                cross_on().start()
-
-        elif gi == 1:
-            chunks(2, send_part)
+    pass_on(2)
+
+    @pl.when(crosses)
+    def _():
+        for part_no in range(2):
+            cross_send(part_no).wait_recv()
+            cross_on(part_no).start()
+        chunks(0, IN_CHUNKS, send_across_y)
+
+    pass_on(4)
+    for gi in range(last):
+        sib_send(0, gi).wait_recv()
+
+    def early_groups(chunk):
+        where(chunk == IN_CHUNKS - 1, lambda: pass_on(REACH))
+        arrived(chunk)
+        for gi in range(last):
+            forward(gi, chunk * heads_chunk)
+
+    chunks(0, IN_CHUNKS, early_groups)
     sib_send(0, last).wait_recv()
-    forward(last, 0)
-
-    def forward_chunk(chunk):
-        arrived(chunk)
-        for gi in range(len(groups)):
-            forward(gi, chunk * heads_chunk)
-
-    chunks(1, forward_chunk)
+    chunks(0, IN_CHUNKS, lambda chunk: forward(last, chunk * heads_chunk))
 
     top = jnp.maximum(jnp.maximum(st_m[0], st_m[1]), st_m[2])
     factors = [jnp.exp2(st_m[gi] - top) for gi in range(len(groups))]
@@ -290,7 +308,7 @@
                     send_sum(gi + 1)
 
             blocks = (ra, rb, 0) if gi == last else (ra, rb)
-            keys_t = jnp.concatenate([key_t[r] for r in blocks], axis=1)
+            keys = jnp.concatenate([kv[r, :, :HEAD_DIM] for r in blocks], axis=0)
             p_all, ds_all, grad_all, query_all = [], [], [], []
             for u in range(heads_step):
                 j = step * heads_step + u
@@ -310,11 +328,11 @@
                 ds_all.append(ds)
                 grad_all.append(dob[:, cols])
                 query_all.append(qb[:, cols])
-                grad_query = nn(keys_t, ds)
+                grad_query = tn(ds, keys)
                 if gi != last:
                     grad_query = grad_query + dq[j]
                 if final:
-                    stage[:, cols] = jnp.transpose(grad_query * SCALE).astype(BF16)
+                    stage[:, cols] = (grad_query * SCALE).astype(BF16)
                 else:
                     dq[j] = grad_query
             p = jnp.concatenate(p_all, axis=1)
@@ -344,7 +362,7 @@
         return ctx_copy(rail_out.at[gi], relay_grads, s_grail.at[gi], r_back.at[0], run_ends[gi])
 
     def grail_home():
-        return ctx_copy(relay_grads, cross_in, s_cross.at[2], r_back.at[1], last_run)
+        return ctx_copy(relay_grads, cross_in, s_cross.at[4], r_back.at[1], last_run)
 
     def cross_back(gi):
         @pl.when(z == Z_CHIPS - 1 - gi)
@@ -387,8 +405,6 @@
         def _():
             grail(rb).start()
 
-    for r in range(REACH + 1):
-        key_t[r] = jnp.transpose(kv[r, :, :HEAD_DIM])
     home[...] = jnp.zeros_like(home)
     for gi in range(last, -1, -1):
         part[...] = jnp.zeros_like(part)
@@ -425,22 +441,27 @@
     mine.start()
 
     all_sent(None)
-    chunks(0, all_sent)
+    chunks(0, IN_CHUNKS, all_sent)
     for j in range(len(groups)):
-        where(jnp.logical_not(ends_run), lambda j=j: rail_send(2 * j).wait_send())
+        where(jnp.logical_not(ends_run), lambda j=j: [rail_send(2 * j, i).wait_send() for i in range(2)])
         sib_send(0, j).wait_send()
         gsib(j).wait_send()
         grail(2 * j + 2).wait_send()
 
     @pl.when(crosses)
     def _():
-        cross_send().wait_send()
-        cross_on().wait_send()
+        for part_no in range(2):
+            cross_send(part_no).wait_send()
+            cross_on(part_no).wait_send()
         grail_home().wait_send()
 
     mine.wait()
     wait_bytes(out_ref.at[:, pl.ds(0, width * (n_head - 1))], s_out)
     wait_bytes(out_ref.at[:, pl.ds(0, width * (n_head - 1))], r_out)
+
+
+def copy_kernel(src_ref, dst_ref):
+    dst_ref[...] = src_ref[...]
 
 
 def per_device(n_head, n_ctx, merged_qkv, out_grads, doc_lengths):
@@ -451,7 +472,7 @@
     dma = pltpu.SemaphoreType.DMA
     n_in = 1 + 2 * IN_CHUNKS
     macs = 5 * GROUP_Q * piece * (REACH + 1) * piece * HEAD_DIM
-    return pl.pallas_call(
+    result = pl.pallas_call(
         functools.partial(kernel, n_head, n_ctx),
         out_shape=jax.ShapeDtypeStruct(merged_qkv.shape, BF16),
         in_specs=[pl.BlockSpec(memory_space=pltpu.SMEM), pl.BlockSpec(memory_space=pl.ANY),
@@ -470,8 +491,7 @@
             pltpu.VMEM((n_groups, GROUP_Q, piece), F32),
             pltpu.VMEM((n_groups, GROUP_Q, piece), F32),
             pltpu.VMEM((GROUP_Q, piece), F32),
-            pltpu.VMEM((REACH + 1, HEAD_DIM, piece), BF16),
-            pltpu.VMEM((GROUP_Q, HEAD_DIM, piece), F32),
+            pltpu.VMEM((GROUP_Q, piece, HEAD_DIM), F32),
             pltpu.VMEM((piece, pair), F32),
             pltpu.VMEM((2, piece, pair), F32),
             pltpu.VMEM((piece, pair), F32),
@@ -484,7 +504,7 @@
             pltpu.VMEM((n_groups, piece, pair), BF16),
             pltpu.VMEM((piece, (GROUP_Q + 2) * HEAD_DIM), BF16),
             dma((n_in,)), dma((n_in,)), dma((n_in,)),
-            dma((n_groups,)), dma((n_groups,)), dma((3,)), dma((1,)), dma((2,)),
+            dma((n_groups, 2)), dma((n_groups, 2)), dma((5,)), dma((2,)), dma((2,)),
             dma((n_groups,)), dma((n_groups,)),
             dma((n_groups,)), dma((n_groups,)),
             dma((n_groups,)), dma((n_groups,)),
@@ -496,6 +516,9 @@
             flops=2 * macs, bytes_accessed=4 * merged_qkv.size * 2,
             transcendentals=GROUP_Q * piece * piece * REACH),
     )(doc_lengths, merged_qkv, out_grads)
+    return pl.pallas_call(
+        copy_kernel, out_shape=jax.ShapeDtypeStruct(result.shape, result.dtype)
+    )(result)
 
 
 def solution(mesh):

time: 76.2 us -> 71.8 us (0.942)
  Pallas kernels: 74 us -> 71.5 us
  local copies, waits for them, and re-layouts: 1.97 us -> 0 us
    pallas_call x1, Pallas kernels: 74 us -> 69.6 us  [per_device(): pl.pallas_call(functools.partial(kernel, n_head, n_ctx), out_shape=jax.Sh...]
    pallas_call x0 -> x1, Pallas kernels: none -> 1.97 us  [per_device(): pl.pallas_call(copy_kernel, out_shape=jax.ShapeDtypeStruct(result.shape,...]
    unnamed x1 -> x0, local copies, waits for them, and re-layouts: 1.97 us -> none
where the time goes in v5:
time: 71.8 us; the launch traced here: 71.6 us
  Pallas kernels  71.5 us (100%)
    pallas_call x1, Pallas kernels, per_device(): pl.pallas_call(functools.partial(kernel, n_head, n_ctx), out_shape=jax.Sh...  69.6 us
    pallas_call x1, Pallas kernels, per_device(): pl.pallas_call(copy_kernel, out_shape=jax.ShapeDtypeStruct(result.shape,...  1.97 us

profile of v5, /device:TPU:1, one launch (start us, length us, event | category | flops | bytes accessed | tf_op | source)
XLA Modules:
  0.0 71.6 jit_solution(13947195174632941457)
XLA Ops:
  0.0 69.6 %shard_map.37.src_ref = bf16[32,10240]{1,0:T(8,128)(2,1)} custom-call(s32[64]{0:T(128)} %lens_ref.1, bf16[32,10240]{1,0:T(8,128)(2,1)} %qkv_ref.1, bf16[32,8192]{1,0:T(8,128)(2,1)} %grads_ref.1), custom_call_target="tpu_custom_call" | custom-call | flops 4697620480 | bytes 2621440 | tf_op jit(solution)/shard_map/pallas_call | solution.py:475
  69.6 2.0 %shard_map.38 = bf16[32,10240]{1,0:T(8,128)(2,1)} custom-call(bf16[32,10240]{1,0:T(8,128)(2,1)} %shard_map.37.src_ref), custom_call_target="tpu_custom_call" | custom-call | tf_op jit(solution)/shard_map/pallas_call | solution.py:519

commit v6 on v5

--- a/solution.py
+++ b/solution.py
@@ -18,6 +18,7 @@
 F32, BF16 = jnp.float32, jnp.bfloat16
 IN_CHUNKS = 4
 HEADS_STEP = 2
+ROWS_STEP = 64
 Z_CHIPS = 8
 
 
@@ -176,8 +177,8 @@
         key_doc[r] = jnp.where(inside, 1.0, 0.0).astype(BF16)
         if r == 0:
             query_doc[...] = jnp.where(inside, 0.0, -FAR).astype(BF16)
-    causal = (lax.broadcasted_iota(jnp.int32, (piece, piece), 0)
-              <= lax.broadcasted_iota(jnp.int32, (piece, piece), 1))
+    row_iota = lax.broadcasted_iota(jnp.int32, (ROWS_STEP, piece), 0)
+    col_iota = lax.broadcasted_iota(jnp.int32, (ROWS_STEP, piece), 1)
 
     def half(part_no):
         return pl.ds(part_no * (piece // 2), piece // 2)
@@ -217,8 +218,8 @@
             cross_send(part_no).start()
 
     pass_on(0)
-    chunks(0, IN_CHUNKS, send_along_x)
-    where(jnp.logical_not(crosses), lambda: chunks(0, IN_CHUNKS, send_across_y))
+    where(crosses, lambda: chunks(0, 2, send_along_x))
+    where(jnp.logical_not(crosses), lambda: chunks(0, IN_CHUNKS, send_all))
 
     groups = ((1, 2), (3, 4), (5, 6))
     last = len(groups) - 1
@@ -240,18 +241,31 @@
             values = jnp.concatenate([kv[r, :, HEAD_DIM:] for r in blocks], axis=0)
             s = nt(keys, query)
             dp = nt(values, grad)
-            if gi == last:
-                s, dp = (jnp.concatenate(
-                    [a[:piece], jnp.where(causal, a[2 * piece:], a[piece:2 * piece])], axis=0)
-                    for a in (s, dp))
-            top = jnp.max(s, axis=0, keepdims=True)
-            p = jnp.exp2(s * TO_EXP2 - top * TO_EXP2)
-            probs[gi, j] = p.astype(BF16)
-            dprobs[gi, j] = dp
+            blocks_of = [pl.ds(i * ROWS_STEP, ROWS_STEP) for i in range(2 * piece // ROWS_STEP)]
+
+            def rows_of(a, i):
+                first = i * ROWS_STEP
+                part_a = a[first:first + ROWS_STEP]
+                if gi == last and first >= piece:
+                    tri = row_iota + (first - piece) <= col_iota
+                    part_a = jnp.where(tri, a[first + piece:first + piece + ROWS_STEP], part_a)
+                return part_a
+
+            s = [rows_of(s, i) for i in range(len(blocks_of))]
+            top = functools.reduce(jnp.maximum, [jnp.max(a, axis=0, keepdims=True) for a in s])
+            top = top * TO_EXP2
+            total_p = total_d = jnp.zeros((1, piece), F32)
+            for i, at in enumerate(blocks_of):
+                dp_i = rows_of(dp, i)
+                p = jnp.exp2(s[i] * TO_EXP2 - top)
+                probs[gi, j, at] = p.astype(BF16)
+                dprobs[gi, j, at] = dp_i
+                total_p = total_p + jnp.sum(p, axis=0, keepdims=True)
+                total_d = total_d + jnp.sum(p * dp_i, axis=0, keepdims=True)
             at = pl.ds(j, 1)
-            st_m[gi, at, :] = top * TO_EXP2
-            st_l[gi, at, :] = jnp.sum(p, axis=0, keepdims=True)
-            st_d[gi, at, :] = jnp.sum(p * dp, axis=0, keepdims=True)
+            st_m[gi, at, :] = top
+            st_l[gi, at, :] = total_p
+            st_d[gi, at, :] = total_d
 
     pass_on(2)
 
@@ -260,7 +274,8 @@
         for part_no in range(2):
             cross_send(part_no).wait_recv()
             cross_on(part_no).start()
-        chunks(0, IN_CHUNKS, send_across_y)
+        chunks(0, 2, send_across_y)
+        chunks(2, IN_CHUNKS, send_all)
 
     pass_on(4)
     for gi in range(last):
@@ -314,16 +329,21 @@
                 j = step * heads_step + u
                 cols = pl.ds(pl.multiple_of(j * HEAD_DIM, HEAD_DIM), HEAD_DIM)
                 at = pl.ds(j, 1)
-                p = probs[gi, j].astype(F32) * gain[gi, at, :]
-                ds = p * (dprobs[gi, j] - delta[at, :])
-                if gi == last:
-                    p_c, ds_c = p[piece:], ds[piece:]
-                    p = jnp.concatenate([p[:piece], jnp.where(causal, 0.0, p_c),
-                                         jnp.where(causal, p_c, 0.0)], axis=0)
-                    ds = jnp.concatenate([ds[:piece], jnp.where(causal, 0.0, ds_c),
-                                          jnp.where(causal, ds_c, 0.0)], axis=0)
-                p = p.astype(BF16)
-                ds = ds.astype(BF16)
+                gain_j, delta_j = gain[gi, at, :], delta[at, :]
+                p, ds, p_own, ds_own = [], [], [], []
+                for i in range(2 * piece // ROWS_STEP):
+                    rows_i = pl.ds(i * ROWS_STEP, ROWS_STEP)
+                    p_i = probs[gi, j, rows_i].astype(F32) * gain_j
+                    ds_i = p_i * (dprobs[gi, j, rows_i] - delta_j)
+                    if gi == last and i * ROWS_STEP >= piece:
+                        tri = row_iota + (i * ROWS_STEP - piece) <= col_iota
+                        p_own.append(jnp.where(tri, p_i, 0.0).astype(BF16))
+                        ds_own.append(jnp.where(tri, ds_i, 0.0).astype(BF16))
+                        p_i, ds_i = jnp.where(tri, 0.0, p_i), jnp.where(tri, 0.0, ds_i)
+                    p.append(p_i.astype(BF16))
+                    ds.append(ds_i.astype(BF16))
+                p = jnp.concatenate(p + p_own, axis=0)
+                ds = jnp.concatenate(ds + ds_own, axis=0)
                 p_all.append(p)
                 ds_all.append(ds)
                 grad_all.append(dob[:, cols])
@@ -460,10 +480,6 @@
     wait_bytes(out_ref.at[:, pl.ds(0, width * (n_head - 1))], r_out)
 
 
-def copy_kernel(src_ref, dst_ref):
-    dst_ref[...] = src_ref[...]
-
-
 def per_device(n_head, n_ctx, merged_qkv, out_grads, doc_lengths):
     rows = merged_qkv.shape[0]
     piece = rows * n_head
@@ -472,7 +488,7 @@
     dma = pltpu.SemaphoreType.DMA
     n_in = 1 + 2 * IN_CHUNKS
     macs = 5 * GROUP_Q * piece * (REACH + 1) * piece * HEAD_DIM
-    result = pl.pallas_call(
+    return pl.pallas_call(
         functools.partial(kernel, n_head, n_ctx),
         out_shape=jax.ShapeDtypeStruct(merged_qkv.shape, BF16),
         in_specs=[pl.BlockSpec(memory_space=pltpu.SMEM), pl.BlockSpec(memory_space=pl.ANY),
@@ -516,9 +532,6 @@
             flops=2 * macs, bytes_accessed=4 * merged_qkv.size * 2,
             transcendentals=GROUP_Q * piece * piece * REACH),
     )(doc_lengths, merged_qkv, out_grads)
-    return pl.pallas_call(
-        copy_kernel, out_shape=jax.ShapeDtypeStruct(result.shape, result.dtype)
-    )(result)
 
 
 def solution(mesh):

time: 71.8 us -> 71.5 us (level)
  Pallas kernels: 71.5 us -> 69.3 us
  local copies, waits for them, and re-layouts: 0 us -> 1.97 us
    pallas_call x1 -> x0, Pallas kernels: 1.97 us -> none  [per_device(): pl.pallas_call(copy_kernel, out_shape=jax.ShapeDtypeStruct(result.shape,...]
    unnamed x0 -> x1, local copies, waits for them, and re-layouts: none -> 1.97 us
where the time goes in v6:
time: 71.5 us; the launch traced here: 71.3 us
  Pallas kernels  69.3 us (97%)
  local copies, waits for them, and re-layouts  1.97 us (3%)
    pallas_call x1, Pallas kernels, per_device(): pl.pallas_call(functools.partial(kernel, n_head, n_ctx), out_shape=jax.Sh...  69.3 us
    unnamed x1, local copies, waits for them, and re-layouts  1.97 us

profile of v6, /device:TPU:1, one launch (start us, length us, event | category | flops | bytes accessed | tf_op | source)
XLA Modules:
  0.0 71.3 jit_solution(16336083878089990797)
XLA Ops:
  0.0 69.3 %shard_map.37 = bf16[32,10240]{1,0:T(8,128)(2,1)} custom-call(s32[64]{0:T(128)} %lens_ref.1, bf16[32,10240]{1,0:T(8,128)(2,1)} %qkv_ref.1, bf16[32,8192]{1,0:T(8,128)(2,1)} %grads_ref.1), custom_call_target="tpu_custom_call" | custom-call | flops 4697620480 | bytes 2621440 | tf_op jit(solution)/shard_map/pallas_call | solution.py:491
  69.4 2.0 %copy.5 = bf16[32,10240]{1,0:T(8,128)(2,1)} copy(bf16[32,10240]{1,0:T(8,128)(2,1)} %shard_map.37) | data formatting | bytes 1310720

commit v7 on v6

--- a/solution.py
+++ b/solution.py
@@ -40,9 +40,9 @@
 
 def kernel(n_head, n_ctx, lens_ref, qkv_ref, grads_ref, out_ref,
            kv, key_doc, query_doc, qb, dob, probs, dprobs, st_m, st_l, st_d, gain, delta,
-           dq, home, part, even, relay_kv, relay_grads, cross_in,
+           dq, home, part, even, cross_in,
            odd_out, odd_in, rail_out, rail_in, stage,
-           s_in, r_in, l_in, s_rail, r_rail, s_cross, r_cross, r_back, s_sib, r_sib,
+           s_in, r_in, l_in, s_rail, r_rail, r_back, s_sib, r_sib,
            s_grail, r_grail, s_gsib, r_gsib, s_out, r_out, l_out):
     rows = qkv_ref.shape[0]
     piece = kv.shape[1]
@@ -61,9 +61,6 @@
         return lax.rem(ctx + n_ctx + 2 * steps, n_ctx)
 
     after, before = shifted(1), shifted(-1)
-    next_run, last_run = shifted(Z_CHIPS), shifted(-Z_CHIPS)
-    run_start = shifted(-z)
-    run_ends = [shifted(Z_CHIPS - 1 - i) for i in range(n_groups)]
     peers = [lax.rem(me + p, n_head) for p in range(1, n_head)]
 
     barrier = pltpu.get_barrier_semaphore()
@@ -80,21 +77,13 @@
         def _():
             body()
 
-    where(jnp.logical_not(starts_run), lambda: greet("ctx", before))
-    where(jnp.logical_not(ends_run), lambda: greet("ctx", after))
-
-    @pl.when(crosses)
-    def _():
-        for other in (next_run, last_run, run_start):
-            greet("ctx", other)
-
-    @pl.when(starts_run)
-    def _():
-        for other in run_ends:
-            greet("ctx", other)
-
-    greeted = len(peers) + 3 + jnp.where(starts_run, n_groups - 1, 0)
-    pl.semaphore_wait(barrier, greeted + jnp.where(ends_run, 2, jnp.where(crosses, 3, 0)))
+    greet("ctx", before)
+    greet("ctx", after)
+    for steps in range(2, n_groups + 1):
+        where(starts_run, lambda: greet("ctx", shifted(-steps)))
+        where(z == Z_CHIPS - steps, lambda: greet("ctx", shifted(steps)))
+    more = jnp.where(starts_run, n_groups - 1, jnp.where(crosses & jnp.logical_not(ends_run), 1, 0))
+    pl.semaphore_wait(barrier, len(peers) + 3 + more)
 
     my_rows = pl.ds(pl.multiple_of(me * rows, rows), rows)
 
@@ -187,15 +176,6 @@
         at, i = half(part_no), r // 2
         return ctx_copy(kv.at[r, at], kv.at[r + 2, at], s_rail.at[i, part_no], r_rail.at[i, part_no], after)
 
-    def cross_send(part_no):
-        at = half(part_no)
-        return ctx_copy(kv.at[0, at], relay_kv.at[at], s_cross.at[part_no], r_cross.at[part_no], next_run)
-
-    def cross_on(part_no):
-        i, at = Z_CHIPS - 1 - z, half(part_no)
-        return ctx_copy(relay_kv.at[at], kv.at[2 * i + 2, at], s_cross.at[2 + part_no],
-                        r_rail.at[i, part_no], run_start)
-
     def sib_send(k, j):
         return ctx_copy(kv.at[2 * j + 2 * k], kv.at[2 * j + 1], s_sib.at[j], r_sib.at[j], sib)
 
@@ -204,7 +184,7 @@
             if r > 0:
                 rail_send(r - 2, part_no).wait_recv()
             if r < REACH:
-                where(jnp.logical_not(ends_run), lambda: rail_send(r, part_no).start())
+                rail_send(r, part_no).start()
         if r < REACH:
             where(core == 0, lambda: sib_send(0, r // 2).start())
         if r > 0:
@@ -212,14 +192,10 @@
 
     arrived(None)
 
-    @pl.when(crosses)
-    def _():
-        for part_no in range(2):
-            cross_send(part_no).start()
-
     pass_on(0)
-    where(crosses, lambda: chunks(0, 2, send_along_x))
-    where(jnp.logical_not(crosses), lambda: chunks(0, IN_CHUNKS, send_all))
+    turn = starts_run | ends_run
+    where(turn, lambda: chunks(0, 2, send_along_x))
+    where(jnp.logical_not(turn), lambda: chunks(0, IN_CHUNKS, send_all))
 
     groups = ((1, 2), (3, 4), (5, 6))
     last = len(groups) - 1
@@ -269,15 +245,9 @@
 
     pass_on(2)
 
-    @pl.when(crosses)
-    def _():
-        for part_no in range(2):
-            cross_send(part_no).wait_recv()
-            cross_on(part_no).start()
-        chunks(0, 2, send_across_y)
-        chunks(2, IN_CHUNKS, send_all)
-
+    where(turn, lambda: chunks(0, 2, send_across_y))
     pass_on(4)
+    where(turn, lambda: chunks(2, IN_CHUNKS, send_all))
     for gi in range(last):
         sib_send(0, gi).wait_recv()
 
@@ -318,8 +288,6 @@
 
                 @pl.when(step == 1)
                 def _():
-                    if final:
-                        cross_back(last)
                     send_sum(gi + 1)
 
             blocks = (ra, rb, 0) if gi == last else (ra, rb)
@@ -378,17 +346,8 @@
         i = r // 2 - 1
         return ctx_copy(rail_out.at[i], rail_in.at[i], s_grail.at[i], r_grail.at[i], before)
 
-    def grail_over(gi):
-        return ctx_copy(rail_out.at[gi], relay_grads, s_grail.at[gi], r_back.at[0], run_ends[gi])
-
-    def grail_home():
-        return ctx_copy(relay_grads, cross_in, s_cross.at[4], r_back.at[1], last_run)
-
-    def cross_back(gi):
-        @pl.when(z == Z_CHIPS - 1 - gi)
-        def _():
-            grail_over(gi).wait_recv()
-            grail_home().start()
+    def grail_home(gi):
+        return ctx_copy(rail_out.at[gi], cross_in, s_grail.at[gi], r_back, shifted(-1 - gi))
 
     def gsib(j):
         return ctx_copy(odd_out.at[j], odd_in.at[j], s_gsib.at[j], r_gsib.at[j], sib)
@@ -419,7 +378,7 @@
 
         @pl.when(starts_run)
         def _():
-            grail_over(gi).start()
+            grail_home(gi).start()
 
         @pl.when(jnp.logical_not(starts_run))
         def _():
@@ -432,9 +391,7 @@
         odd_out[gi] = (part[0] * key_scale()).astype(BF16)
         gsib(gi).start()
         even[...] = part[1] * key_scale()
-    cross_back(1)
     send_sum(0)
-    cross_back(0)
 
     home[...] = home[...] * key_scale()
 
@@ -450,7 +407,7 @@
 
     @pl.when(crosses)
     def _():
-        grail_home().wait_recv()
+        grail_home(0).wait_recv()
         home[...] += cross_in[...].astype(F32)
 
     own = home[...]
@@ -463,17 +420,11 @@
     all_sent(None)
     chunks(0, IN_CHUNKS, all_sent)
     for j in range(len(groups)):
-        where(jnp.logical_not(ends_run), lambda j=j: [rail_send(2 * j, i).wait_send() for i in range(2)])
+        rail_send(2 * j, 0).wait_send()
+        rail_send(2 * j, 1).wait_send()
         sib_send(0, j).wait_send()
         gsib(j).wait_send()
         grail(2 * j + 2).wait_send()
-
-    @pl.when(crosses)
-    def _():
-        for part_no in range(2):
-            cross_send(part_no).wait_send()
-            cross_on(part_no).wait_send()
-        grail_home().wait_send()
 
     mine.wait()
     wait_bytes(out_ref.at[:, pl.ds(0, width * (n_head - 1))], s_out)
@@ -512,15 +463,13 @@
             pltpu.VMEM((2, piece, pair), F32),
             pltpu.VMEM((piece, pair), F32),
             pltpu.VMEM((piece, pair), BF16),
-            pltpu.VMEM((piece, pair), BF16),
-            pltpu.VMEM((piece, pair), BF16),
             pltpu.VMEM((n_groups, piece, pair), BF16),
             pltpu.VMEM((n_groups, piece, pair), BF16),
             pltpu.VMEM((n_groups, piece, pair), BF16),
             pltpu.VMEM((n_groups, piece, pair), BF16),
             pltpu.VMEM((piece, (GROUP_Q + 2) * HEAD_DIM), BF16),
             dma((n_in,)), dma((n_in,)), dma((n_in,)),
-            dma((n_groups, 2)), dma((n_groups, 2)), dma((5,)), dma((2,)), dma((2,)),
+            dma((n_groups, 2)), dma((n_groups, 2)), dma,
             dma((n_groups,)), dma((n_groups,)),
             dma((n_groups,)), dma((n_groups,)),
             dma((n_groups,)), dma((n_groups,)),

time: 71.5 us -> 82.2 us (1.15)
  Pallas kernels: 69.3 us -> 80 us
    pallas_call x1, Pallas kernels: 69.3 us -> 80 us  [per_device(): pl.pallas_call(functools.partial(kernel, n_head, n_ctx), out_shape=jax.Sh...]
where the time goes in v7:
time: 82.2 us; the launch traced here: 82 us
  Pallas kernels  80 us (97%)
  local copies, waits for them, and re-layouts  1.97 us (2%)
    pallas_call x1, Pallas kernels, per_device(): pl.pallas_call(functools.partial(kernel, n_head, n_ctx), out_shape=jax.Sh...  80 us
    unnamed x1, local copies, waits for them, and re-layouts  1.97 us

profile of v7, /device:TPU:1, one launch (start us, length us, event | category | flops | bytes accessed | tf_op | source)
XLA Modules:
  0.0 82.0 jit_solution(5825874319504167266)
XLA Ops:
  0.0 80.0 %shard_map.37 = bf16[32,10240]{1,0:T(8,128)(2,1)} custom-call(s32[64]{0:T(128)} %lens_ref.1, bf16[32,10240]{1,0:T(8,128)(2,1)} %qkv_ref.1, bf16[32,8192]{1,0:T(8,128)(2,1)} %grads_ref.1), custom_call_target="tpu_custom_call" | custom-call | flops 4697620480 | bytes 2621440 | tf_op jit(solution)/shard_map/pallas_call | solution.py:442
  80.0 2.0 %copy.5 = bf16[32,10240]{1,0:T(8,128)(2,1)} copy(bf16[32,10240]{1,0:T(8,128)(2,1)} %shard_map.37) | data formatting | bytes 1310720

commit v8 on v6

--- a/solution.py
+++ b/solution.py
@@ -40,7 +40,7 @@
 
 def kernel(n_head, n_ctx, lens_ref, qkv_ref, grads_ref, out_ref,
            kv, key_doc, query_doc, qb, dob, probs, dprobs, st_m, st_l, st_d, gain, delta,
-           dq, home, part, even, relay_kv, relay_grads, cross_in,
+           dq, home, part, even, relay_kv, cross_in,
            odd_out, odd_in, rail_out, rail_in, stage,
            s_in, r_in, l_in, s_rail, r_rail, s_cross, r_cross, r_back, s_sib, r_sib,
            s_grail, r_grail, s_gsib, r_gsib, s_out, r_out, l_out):
@@ -85,16 +85,16 @@
 
     @pl.when(crosses)
     def _():
-        for other in (next_run, last_run, run_start):
+        for other in (next_run, last_run, run_start, shifted(Z_CHIPS - z)):
             greet("ctx", other)
 
     @pl.when(starts_run)
     def _():
-        for other in run_ends:
+        for other in run_ends + [shifted(-1 - i) for i in range(n_groups)]:
             greet("ctx", other)
 
-    greeted = len(peers) + 3 + jnp.where(starts_run, n_groups - 1, 0)
-    pl.semaphore_wait(barrier, greeted + jnp.where(ends_run, 2, jnp.where(crosses, 3, 0)))
+    more = jnp.where(starts_run, 2 * n_groups - 1, jnp.where(ends_run, 3, jnp.where(crosses, 4, 0)))
+    pl.semaphore_wait(barrier, len(peers) + 3 + more)
 
     my_rows = pl.ds(pl.multiple_of(me * rows, rows), rows)
 
@@ -124,18 +124,11 @@
                     send_sem=s_in.at[i], recv_sem=r_in.at[i],
                     device_id={"head": peer}, device_id_type=MESH).start()
 
-    def send_along_x(chunk):
+    def send_all(chunk):
         for src, src_cols, dst, dst_cols, i in sends(chunk):
             pltpu.make_async_copy(
                 src.at[:, src_cols(me)], dst.at[my_rows, dst_cols], l_in.at[i]).start()
-        send_to(chunk, peers[1::2])
-
-    def send_across_y(chunk):
-        send_to(chunk, peers[0::2])
-
-    def send_all(chunk):
-        send_along_x(chunk)
-        send_across_y(chunk)
+        send_to(chunk, peers)
 
     def arrived(chunk):
         for src, src_cols, dst, dst_cols, i in sends(chunk):
@@ -218,7 +211,6 @@
             cross_send(part_no).start()
 
     pass_on(0)
-    where(crosses, lambda: chunks(0, 2, send_along_x))
     where(jnp.logical_not(crosses), lambda: chunks(0, IN_CHUNKS, send_all))
 
     groups = ((1, 2), (3, 4), (5, 6))
@@ -274,8 +266,7 @@
         for part_no in range(2):
             cross_send(part_no).wait_recv()
             cross_on(part_no).start()
-        chunks(0, 2, send_across_y)
-        chunks(2, IN_CHUNKS, send_all)
+        chunks(0, IN_CHUNKS, send_all)
 
     pass_on(4)
     for gi in range(last):
@@ -318,8 +309,6 @@
 
                 @pl.when(step == 1)
                 def _():
-                    if final:
-                        cross_back(last)
                     send_sum(gi + 1)
 
             blocks = (ra, rb, 0) if gi == last else (ra, rb)
@@ -378,17 +367,8 @@
         i = r // 2 - 1
         return ctx_copy(rail_out.at[i], rail_in.at[i], s_grail.at[i], r_grail.at[i], before)
 
-    def grail_over(gi):
-        return ctx_copy(rail_out.at[gi], relay_grads, s_grail.at[gi], r_back.at[0], run_ends[gi])
-
-    def grail_home():
-        return ctx_copy(relay_grads, cross_in, s_cross.at[4], r_back.at[1], last_run)
-
-    def cross_back(gi):
-        @pl.when(z == Z_CHIPS - 1 - gi)
-        def _():
-            grail_over(gi).wait_recv()
-            grail_home().start()
+    def grail_home(gi):
+        return ctx_copy(rail_out.at[gi], cross_in, s_grail.at[gi], r_back, shifted(-1 - gi))
 
     def gsib(j):
         return ctx_copy(odd_out.at[j], odd_in.at[j], s_gsib.at[j], r_gsib.at[j], sib)
@@ -419,7 +399,7 @@
 
         @pl.when(starts_run)
         def _():
-            grail_over(gi).start()
+            grail_home(gi).start()
 
         @pl.when(jnp.logical_not(starts_run))
         def _():
@@ -432,9 +412,7 @@
         odd_out[gi] = (part[0] * key_scale()).astype(BF16)
         gsib(gi).start()
         even[...] = part[1] * key_scale()
-    cross_back(1)
     send_sum(0)
-    cross_back(0)
 
     home[...] = home[...] * key_scale()
 
@@ -450,7 +428,7 @@
 
     @pl.when(crosses)
     def _():
-        grail_home().wait_recv()
+        grail_home(0).wait_recv()
         home[...] += cross_in[...].astype(F32)
 
     own = home[...]
@@ -473,7 +451,6 @@
         for part_no in range(2):
             cross_send(part_no).wait_send()
             cross_on(part_no).wait_send()
-        grail_home().wait_send()
 
     mine.wait()
     wait_bytes(out_ref.at[:, pl.ds(0, width * (n_head - 1))], s_out)
@@ -513,14 +490,13 @@
             pltpu.VMEM((piece, pair), F32),
             pltpu.VMEM((piece, pair), BF16),
             pltpu.VMEM((piece, pair), BF16),
-            pltpu.VMEM((piece, pair), BF16),
             pltpu.VMEM((n_groups, piece, pair), BF16),
             pltpu.VMEM((n_groups, piece, pair), BF16),
             pltpu.VMEM((n_groups, piece, pair), BF16),
             pltpu.VMEM((n_groups, piece, pair), BF16),
             pltpu.VMEM((piece, (GROUP_Q + 2) * HEAD_DIM), BF16),
             dma((n_in,)), dma((n_in,)), dma((n_in,)),
-            dma((n_groups, 2)), dma((n_groups, 2)), dma((5,)), dma((2,)), dma((2,)),
+            dma((n_groups, 2)), dma((n_groups, 2)), dma((4,)), dma((2,)), dma,
             dma((n_groups,)), dma((n_groups,)),
             dma((n_groups,)), dma((n_groups,)),
             dma((n_groups,)), dma((n_groups,)),

time: 71.5 us -> 77.1 us (1.078)
  Pallas kernels: 69.3 us -> 74.9 us
    pallas_call x1, Pallas kernels: 69.3 us -> 74.9 us  [per_device(): pl.pallas_call(functools.partial(kernel, n_head, n_ctx), out_shape=jax.Sh...]
where the time goes in v8:
time: 77.1 us; the launch traced here: 76.9 us
  Pallas kernels  74.9 us (97%)
  local copies, waits for them, and re-layouts  1.97 us (3%)
    pallas_call x1, Pallas kernels, per_device(): pl.pallas_call(functools.partial(kernel, n_head, n_ctx), out_shape=jax.Sh...  74.9 us
    unnamed x1, local copies, waits for them, and re-layouts  1.97 us

profile of v8, /device:TPU:1, one launch (start us, length us, event | category | flops | bytes accessed | tf_op | source)
XLA Modules:
  0.0 76.9 jit_solution(13609262217148763084)
XLA Ops:
  0.0 74.9 %shard_map.37 = bf16[32,10240]{1,0:T(8,128)(2,1)} custom-call(s32[64]{0:T(128)} %lens_ref.1, bf16[32,10240]{1,0:T(8,128)(2,1)} %qkv_ref.1, bf16[32,8192]{1,0:T(8,128)(2,1)} %grads_ref.1), custom_call_target="tpu_custom_call" | custom-call | flops 4697620480 | bytes 2621440 | tf_op jit(solution)/shard_map/pallas_call | solution.py:468
  74.9 2.0 %copy.5 = bf16[32,10240]{1,0:T(8,128)(2,1)} copy(bf16[32,10240]{1,0:T(8,128)(2,1)} %shard_map.37) | data formatting | bytes 1310720

commit v9 on v8

--- a/solution.py
+++ b/solution.py
@@ -124,11 +124,18 @@
                     send_sem=s_in.at[i], recv_sem=r_in.at[i],
                     device_id={"head": peer}, device_id_type=MESH).start()
 
-    def send_all(chunk):
+    def send_along_x(chunk):
         for src, src_cols, dst, dst_cols, i in sends(chunk):
             pltpu.make_async_copy(
                 src.at[:, src_cols(me)], dst.at[my_rows, dst_cols], l_in.at[i]).start()
-        send_to(chunk, peers)
+        send_to(chunk, peers[1::2])
+
+    def send_across_y(chunk):
+        send_to(chunk, peers[0::2])
+
+    def send_all(chunk):
+        send_along_x(chunk)
+        send_across_y(chunk)
 
     def arrived(chunk):
         for src, src_cols, dst, dst_cols, i in sends(chunk):
@@ -211,6 +218,7 @@
             cross_send(part_no).start()
 
     pass_on(0)
+    where(crosses, lambda: chunks(0, 2, send_along_x))
     where(jnp.logical_not(crosses), lambda: chunks(0, IN_CHUNKS, send_all))
 
     groups = ((1, 2), (3, 4), (5, 6))
@@ -266,7 +274,8 @@
         for part_no in range(2):
             cross_send(part_no).wait_recv()
             cross_on(part_no).start()
-        chunks(0, IN_CHUNKS, send_all)
+        chunks(0, 2, send_across_y)
+        chunks(2, IN_CHUNKS, send_all)
 
     pass_on(4)
     for gi in range(last):

time: 77.1 us -> 77.1 us (level)
  no operation moved by 1% of the time
where the time goes in v9:
time: 77.1 us; the launch traced here: 76.9 us
  Pallas kernels  74.9 us (97%)
  local copies, waits for them, and re-layouts  1.97 us (3%)
    pallas_call x1, Pallas kernels, per_device(): pl.pallas_call(functools.partial(kernel, n_head, n_ctx), out_shape=jax.Sh...  74.9 us
    unnamed x1, local copies, waits for them, and re-layouts  1.97 us

profile of v9, /device:TPU:1, one launch (start us, length us, event | category | flops | bytes accessed | tf_op | source)
XLA Modules:
  0.0 76.9 jit_solution(5226394948026479366)
XLA Ops:
  0.0 74.9 %shard_map.37 = bf16[32,10240]{1,0:T(8,128)(2,1)} custom-call(s32[64]{0:T(128)} %lens_ref.1, bf16[32,10240]{1,0:T(8,128)(2,1)} %qkv_ref.1, bf16[32,8192]{1,0:T(8,128)(2,1)} %grads_ref.1), custom_call_target="tpu_custom_call" | custom-call | flops 4697620480 | bytes 2621440 | tf_op jit(solution)/shard_map/pallas_call | solution.py:477
  74.9 2.0 %copy.5 = bf16[32,10240]{1,0:T(8,128)(2,1)} copy(bf16[32,10240]{1,0:T(8,128)(2,1)} %shard_map.37) | data formatting | bytes 1310720
